TPU v7x, 32 devices: a whole 2x2x4 slice. The times are simulated.
32 devices in a mesh: row: 8 (over z, x), col: 4 (over y, core).
Axes of the slice: x: 2, y: 2, z: 4, core: 2. Of those that a mesh axis runs over, the one named last changes fastest.
Arguments:
- query_nope: bfloat16 [8, 128, 128], P(None, 'row'), may hold values from -9 to 9
- query_rope: bfloat16 [8, 128, 64], P(None, 'row'), may hold values from -10 to 80
- key_up_weight: bfloat16 [128, 128, 512], P('row'), may hold values from -0.5 to 0.5
- value_up_weight: bfloat16 [128, 512, 128], P('row'), may hold values from -0.25 to 0.25
- latent_cache: bfloat16 [131072, 576], P(('row', 'col')), may hold values from -6 to 6
- lengths: int32 [8], replicated, may hold values from 1 to 16384, as said below
- page_table: int32 [8, 256], replicated, may hold values from -1 to 2047, as said below
Outputs:
- head_values: bfloat16 [8, 16384], P(None, 'row')
Inputs may be any that keep to these rules, and one draw needn't show every extreme that they name: `lengths`: the largest length is exactly 16384. `page_table`: entry (r, p) is -1 exactly when p * 64 >= lengths[r]; all other entries are distinct cache pages, page k lying on the device of index k // 64 along row+col.
All inputs are finite; a program needn't handle non-finite values.
Results may differ from a plain program's by a relative error of at most 0.0094.
Values may be sent and summed in bfloat16 or wider, within the bound.
A program may use at most 128 MiB of HBM per device.

v0:
```python
import jax
import jax.numpy as jnp
from jax import lax
from jax.sharding import PartitionSpec as P

HEAD_NOPE_WIDTH = 128
ROTARY_WIDTH = 64
PAGE = 64


MASKED = -1e30


def merged(array, axis, combine):
    everything = jax.tree.map(lambda part: lax.all_gather(part, axis), array)
    first = jax.tree.map(lambda part: part[0], everything)

    def merged_step(k, so_far):
        return combine(so_far, jax.tree.map(lambda part: part[k], everything))

    return lax.fori_loop(1, lax.axis_size(axis), merged_step, first)


def combine(first, second):
    top_first, denom_first, latent_first = first
    top_second, denom_second, latent_second = second
    top = jnp.maximum(top_first, top_second)
    weight_first = jnp.exp(top_first - top)
    weight_second = jnp.exp(top_second - top)
    denom = weight_first * denom_first + weight_second * denom_second
    latent_rows = weight_first[..., None] * latent_first + weight_second[..., None] * latent_second
    return (top, denom, latent_rows)


def fold_sources(top_parts, denom_parts, latent_parts):
    joint_top = jnp.max(top_parts, axis=0)
    source_weight = jnp.exp(top_parts - joint_top[None])
    joint_denom = jnp.sum(source_weight * denom_parts, axis=0)
    joint_latent = jnp.sum(source_weight[..., None] * latent_parts, axis=0)
    return (joint_top, joint_denom, joint_latent)


def local(
    query_nope, query_rope, key_up_weight, value_up_weight, latent_cache, lengths, page_table
):
    scale = float(HEAD_NOPE_WIDTH + ROTARY_WIDTH) ** (-0.5)
    requests, local_heads, _ = query_nope.shape
    kv_width = key_up_weight.shape[2]
    width = latent_cache.shape[1]
    query_latent = jnp.einsum(
        "rhn,hnc->rhc", query_nope, key_up_weight, preferred_element_type=jnp.float32
    ).astype(jnp.bfloat16)
    query = jnp.concatenate([query_latent, query_rope], axis=2)
    queries = lax.all_gather(query, "row", axis=1, tiled=True)
    heads = queries.shape[1]
    slots = latent_cache.shape[0] // PAGE
    table_width = page_table.shape[1]
    device = lax.axis_index("row") * lax.axis_size("col") + lax.axis_index("col")
    local_slot = page_table - device * slots
    matches = local_slot[:, :, None] == jnp.arange(slots, dtype=jnp.int32)[None, None, :]
    owned = jnp.any(matches, axis=1)
    page_index = jnp.sum(
        jnp.where(matches, jnp.arange(table_width, dtype=jnp.int32)[None, :, None], 0), axis=(0, 1)
    )
    limit = jnp.sum(jnp.where(owned, lengths[:, None], 0), axis=0)
    position = page_index[:, None] * PAGE + jnp.arange(PAGE, dtype=jnp.int32)[None, :]
    valid = position < limit[:, None]
    group = 8
    blocks = slots // group
    block_keys = latent_cache.reshape(blocks, group, PAGE, width)
    block_valid = valid.reshape(blocks, group, PAGE)
    block_owned = jnp.transpose(owned.reshape(requests, blocks, group), (1, 0, 2))

    def body_step(carry, items):
        top, denom, latent_rows = carry
        key_rows, live, owner = items
        slot_query = jnp.einsum(
            "rs,rhd->shd", owner.astype(jnp.bfloat16), queries, preferred_element_type=jnp.float32
        ).astype(jnp.bfloat16)
        scores = (
            jnp.einsum("shd,std->sht", slot_query, key_rows, preferred_element_type=jnp.float32)
            * scale
        )
        scores = jnp.where(live[:, None, :], scores, MASKED)
        slot_top = jnp.max(scores, axis=2)
        expo = jnp.where(live[:, None, :], jnp.exp(scores - slot_top[:, :, None]), 0.0).astype(
            jnp.bfloat16
        )
        slot_denom = jnp.sum(expo.astype(jnp.float32), axis=2)
        slot_latent = jnp.einsum(
            "sht,stc->shc", expo, key_rows[:, :, :kv_width], preferred_element_type=jnp.float32
        )
        candidate = jnp.where(owner[:, :, None], slot_top[None, :, :], MASKED)
        new_top = jnp.maximum(top, jnp.max(candidate, axis=1))
        keep = jnp.exp(top - new_top)
        weight = jnp.where(
            owner[:, :, None], jnp.exp(slot_top[None, :, :] - new_top[:, None, :]), 0.0
        )
        denom = denom * keep + jnp.sum(weight * slot_denom[None, :, :], axis=1)
        latent_rows = latent_rows * keep[..., None] + jnp.einsum(
            "rsh,shc->rhc", weight, slot_latent, precision=lax.Precision.HIGHEST
        )
        return ((new_top, denom, latent_rows), None)

    start_carry = (
        jnp.full((requests, heads), MASKED, jnp.float32),
        jnp.zeros((requests, heads), jnp.float32),
        jnp.zeros((requests, heads, kv_width), jnp.float32),
    )
    partials, _ = lax.scan(body_step, start_carry, (block_keys, block_valid, block_owned))
    sources = lax.axis_size("row")
    top_parts, denom_parts, latent_parts = (
        lax.all_to_all(partials[0], "row", split_axis=1, concat_axis=0, tiled=True),
        lax.all_to_all(partials[1], "row", split_axis=1, concat_axis=0, tiled=True),
        lax.all_to_all(partials[2], "row", split_axis=1, concat_axis=0, tiled=True),
    )
    row_part = fold_sources(
        top_parts.reshape(sources, requests, local_heads),
        denom_parts.reshape(sources, requests, local_heads),
        latent_parts.reshape(sources, requests, local_heads, kv_width),
    )
    _, denom, latent_rows = merged(row_part, "col", combine)
    attended = (latent_rows / denom[..., None]).astype(jnp.bfloat16)
    values = jnp.einsum(
        "rhc,hcv->rhv", attended, value_up_weight, preferred_element_type=jnp.float32
    )
    return values.astype(jnp.bfloat16).reshape(requests, local_heads * value_up_weight.shape[2])


def solution(mesh):
    placed = (
        P(None, "row", None),
        P(None, "row", None),
        P("row", None, None),
        P("row", None, None),
        P(("row", "col"), None),
        P(),
        P(),
    )
    return jax.shard_map(
        local, mesh=mesh, in_specs=placed, out_specs=P(None, "row"), check_vma=False
    )
```

profile of v0, /device:TPU:0, one launch (start us, length us, event | category | flops | bytes accessed | tf_op | source)
XLA Modules:
  0.0 290.7 jit_solution(11976586689150297596)
XLA Ops:
  11.4 7.6 %copy.96 = bf16[4096,576]{1,0:T(8,128)(2,1)} copy(bf16[4096,576]{0,1:T(8,128)(2,1)} %param.15) | data formatting | bytes 9437184 | tf_op args[4]
  19.1 35.8 %all-gather.6.cloned.1.call-done = bf16[8,128,576]{2,0,1:T(8,128)(2,1)} async-done(((bf16[8,16,576]{2,0,1:T(8,128)(2,1)}), bf16[8,128,576]{2,0,1:T(8,128)(2,1)}) %all-gather.6.cloned.1.call-update) | async-done | bytes 1179664 | tf_op jit(solution)/shard_map/all_gather | solution.py:54
  54.9 2.6 copy.98
  57.5 131.6 %while.35 = (s32[]{:T(128)}, f32[8,128]{0,1:T(8,128)S(1)}, f32[8,128]{0,1:T(8,128)}, f32[8,128,512]{2,0,1:T(8,128)}, pred[8,8,8]{2,1,0:T(8,128)(4,1)}, /*index=5...) while((s32[]{:T(128)}, f32[8,128]{0,1:T(8,128)S(1)}, ...), condition=%wide.region_8.9_spmd.clone, body=%wide.region_3.8_spmd.clone.sunk | while | flops 205327360 | bytes 16208913 | solution.py:110
  57.6 1.2 convolution_convert_fusion.4
  58.8 1.2 dynamic-slice_bitcast_fusion.6
  61.1 2.1 fusion.60
  66.5 6.3 %bitcast_add_fusion.2 = f32[8,128,512]{2,0,1:T(8,128)} fusion(f32[8,128,512]{2,0,1:T(8,128)} %get-tuple-element.481, f32[8,128,512]{2,1,0:T(8,128)} %fusion.60, f32[8,128]{0,1:T(8,128)S(1)} %get-tuple-element.467, pred[]{:T(512)S(6)} %compare.3, f32[8,128]{0,1:T(8,128)S(1)} %select_maximum_fusion.2, f32[8,128]{0,1:T(8,128)S(1)} %copy.141, ...), kind=kOutput, calls=%fused_computation.8.clone.1 | convolution fusion | flops 51920896 | bytes 6303809 | tf_op jit(solution)/shard_map/while/body/eval_jaxpr/rsh,shc->rhc/dot_general | solution.py:100
  72.7 1.2 convolution_convert_fusion.4
  74.0 1.2 dynamic-slice_bitcast_fusion.6
  76.3 2.1 fusion.60
  81.0 1.5 fusion.59
  82.5 6.9 %bitcast_add_fusion.2 = f32[8,128,512]{2,0,1:T(8,128)} fusion(f32[8,128,512]{2,0,1:T(8,128)} %get-tuple-element.481, f32[8,128,512]{2,1,0:T(8,128)} %fusion.60, f32[8,128]{0,1:T(8,128)S(1)} %get-tuple-element.467, pred[]{:T(512)S(6)} %compare.3, f32[8,128]{0,1:T(8,128)S(1)} %select_maximum_fusion.2, f32[8,128]{0,1:T(8,128)S(1)} %copy.141, ...), kind=kOutput, calls=%fused_computation.8.clone.1 | convolution fusion | flops 51920896 | bytes 6303809 | tf_op jit(solution)/shard_map/while/body/eval_jaxpr/rsh,shc->rhc/dot_general | solution.py:100
  89.4 1.2 convolution_convert_fusion.4
  92.9 2.1 fusion.60
  97.6 1.5 fusion.59
  99.1 6.9 %bitcast_add_fusion.2 = f32[8,128,512]{2,0,1:T(8,128)} fusion(f32[8,128,512]{2,0,1:T(8,128)} %get-tuple-element.481, f32[8,128,512]{2,1,0:T(8,128)} %fusion.60, f32[8,128]{0,1:T(8,128)S(1)} %get-tuple-element.467, pred[]{:T(512)S(6)} %compare.3, f32[8,128]{0,1:T(8,128)S(1)} %select_maximum_fusion.2, f32[8,128]{0,1:T(8,128)S(1)} %copy.141, ...), kind=kOutput, calls=%fused_computation.8.clone.1 | convolution fusion | flops 51920896 | bytes 6303809 | tf_op jit(solution)/shard_map/while/body/eval_jaxpr/rsh,shc->rhc/dot_general | solution.py:100
  106.0 1.2 convolution_convert_fusion.4
  109.5 2.1 fusion.60
  114.2 1.5 fusion.59
  115.7 6.9 %bitcast_add_fusion.2 = f32[8,128,512]{2,0,1:T(8,128)} fusion(f32[8,128,512]{2,0,1:T(8,128)} %get-tuple-element.481, f32[8,128,512]{2,1,0:T(8,128)} %fusion.60, f32[8,128]{0,1:T(8,128)S(1)} %get-tuple-element.467, pred[]{:T(512)S(6)} %compare.3, f32[8,128]{0,1:T(8,128)S(1)} %select_maximum_fusion.2, f32[8,128]{0,1:T(8,128)S(1)} %copy.141, ...), kind=kOutput, calls=%fused_computation.8.clone.1 | convolution fusion | flops 51920896 | bytes 6303809 | tf_op jit(solution)/shard_map/while/body/eval_jaxpr/rsh,shc->rhc/dot_general | solution.py:100
  122.6 1.2 convolution_convert_fusion.4
  126.2 2.1 fusion.60
  130.9 1.5 fusion.59
  132.4 6.9 %bitcast_add_fusion.2 = f32[8,128,512]{2,0,1:T(8,128)} fusion(f32[8,128,512]{2,0,1:T(8,128)} %get-tuple-element.481, f32[8,128,512]{2,1,0:T(8,128)} %fusion.60, f32[8,128]{0,1:T(8,128)S(1)} %get-tuple-element.467, pred[]{:T(512)S(6)} %compare.3, f32[8,128]{0,1:T(8,128)S(1)} %select_maximum_fusion.2, f32[8,128]{0,1:T(8,128)S(1)} %copy.141, ...), kind=kOutput, calls=%fused_computation.8.clone.1 | convolution fusion | flops 51920896 | bytes 6303809 | tf_op jit(solution)/shard_map/while/body/eval_jaxpr/rsh,shc->rhc/dot_general | solution.py:100
  139.3 1.2 convolution_convert_fusion.4
  142.8 2.1 fusion.60
  147.5 1.5 fusion.59
  149.0 6.9 %bitcast_add_fusion.2 = f32[8,128,512]{2,0,1:T(8,128)} fusion(f32[8,128,512]{2,0,1:T(8,128)} %get-tuple-element.481, f32[8,128,512]{2,1,0:T(8,128)} %fusion.60, f32[8,128]{0,1:T(8,128)S(1)} %get-tuple-element.467, pred[]{:T(512)S(6)} %compare.3, f32[8,128]{0,1:T(8,128)S(1)} %select_maximum_fusion.2, f32[8,128]{0,1:T(8,128)S(1)} %copy.141, ...), kind=kOutput, calls=%fused_computation.8.clone.1 | convolution fusion | flops 51920896 | bytes 6303809 | tf_op jit(solution)/shard_map/while/body/eval_jaxpr/rsh,shc->rhc/dot_general | solution.py:100
  155.9 1.2 convolution_convert_fusion.4
  159.4 2.1 fusion.60
  164.1 1.5 fusion.59
  165.6 6.9 %bitcast_add_fusion.2 = f32[8,128,512]{2,0,1:T(8,128)} fusion(f32[8,128,512]{2,0,1:T(8,128)} %get-tuple-element.481, f32[8,128,512]{2,1,0:T(8,128)} %fusion.60, f32[8,128]{0,1:T(8,128)S(1)} %get-tuple-element.467, pred[]{:T(512)S(6)} %compare.3, f32[8,128]{0,1:T(8,128)S(1)} %select_maximum_fusion.2, f32[8,128]{0,1:T(8,128)S(1)} %copy.141, ...), kind=kOutput, calls=%fused_computation.8.clone.1 | convolution fusion | flops 51920896 | bytes 6303809 | tf_op jit(solution)/shard_map/while/body/eval_jaxpr/rsh,shc->rhc/dot_general | solution.py:100
  172.6 1.2 convolution_convert_fusion.4
  176.1 2.1 fusion.60
  180.8 1.5 fusion.59
  182.3 6.9 %bitcast_add_fusion.2 = f32[8,128,512]{2,0,1:T(8,128)} fusion(f32[8,128,512]{2,0,1:T(8,128)} %get-tuple-element.481, f32[8,128,512]{2,1,0:T(8,128)} %fusion.60, f32[8,128]{0,1:T(8,128)S(1)} %get-tuple-element.467, pred[]{:T(512)S(6)} %compare.3, f32[8,128]{0,1:T(8,128)S(1)} %select_maximum_fusion.2, f32[8,128]{0,1:T(8,128)S(1)} %copy.141, ...), kind=kOutput, calls=%fused_computation.8.clone.1 | convolution fusion | flops 51920896 | bytes 6303809 | tf_op jit(solution)/shard_map/while/body/eval_jaxpr/rsh,shc->rhc/dot_general | solution.py:100
  189.9 3.3 %all-to-all-start = ((f32[8,1,128]{2,1,0:T(1,128)}), f32[8,1,128]{2,1,0:T(1,128)S(1)}, u32[]{:S(2)}, u32[]{:S(2)}) async-start(f32[8,1,128]{2,1,0:T(1,128)} %reshape.72), calls=%async_computation | async-start | bytes 8192 | tf_op jit(solution)/shard_map/all_to_all | solution.py:113
  194.3 5.3 %all-to-all-done = f32[8,1,128]{2,1,0:T(1,128)S(1)} async-done(((f32[8,1,128]{2,1,0:T(1,128)}), f32[8,1,128]{2,1,0:T(1,128)S(1)}, u32[]{:S(2)}, u32[]{:S(2)}) %all-to-all-start) | async-done | bytes 4128 | tf_op jit(solution)/shard_map/all_to_all | solution.py:113
  199.6 8.8 %all_to_all.47 = f32[8,1,128]{2,1,0:T(1,128)S(1)} all-to-all(f32[8,1,128]{2,1,0:T(1,128)S(1)} %reshape.74), channel_id=1, replica_groups=mesh['row'=8,'col'=4] {'row'}, dimensions={0} | all-to-all | bytes 8192 | tf_op jit(solution)/shard_map/all_to_all | solution.py:114
  208.4 4.3 %all-to-all-start.2 = ((f32[8,128,512]{2,0,1:T(8,128)}), f32[8,128,512]{2,0,1:T(8,128)}, u32[]{:S(2)}, u32[]{:S(2)}) async-start(f32[8,128,512]{2,0,1:T(8,128)} %get-tuple-element.228), calls=%async_computation.2 | async-start | bytes 4194304 | tf_op jit(solution)/shard_map/all_to_all | solution.py:115
  214.9 43.4 %all-to-all-done.2 = f32[8,128,512]{2,0,1:T(8,128)} async-done(((f32[8,128,512]{2,0,1:T(8,128)}), f32[8,128,512]{2,0,1:T(8,128)}, u32[]{:S(2)}, u32[]{:S(2)}) %all-to-all-start.2) | async-done | bytes 2097184 | tf_op jit(solution)/shard_map/all_to_all | solution.py:115
  258.3 1.8 multiply_reduce_fusion.1
  261.0 5.2 %all-gather.1 = f32[32,16]{1,0:T(8,128)S(1)} all-gather(f32[8,16]{1,0:T(8,128)S(1)} %get-tuple-element.356), channel_id=3, replica_groups=mesh['row'=8,'col'=4] {'col'}, dimensions={0}, use_global_device_ids=true | all-gather | bytes 2560 | tf_op jit(solution)/shard_map/all_gather | solution.py:15
  266.2 5.2 %all-gather = f32[32,16]{1,0:T(8,128)S(1)} all-gather(f32[8,16]{1,0:T(8,128)S(1)} %bitcast_reduce_fusion), channel_id=2, replica_groups=mesh['row'=8,'col'=4] {'col'}, dimensions={0}, use_global_device_ids=true | all-gather | bytes 2560 | tf_op jit(solution)/shard_map/all_gather | solution.py:15
  271.4 5.4 %all-gather.8.cloned.1.call-done = f32[32,16,512]{2,1,0:T(8,128)} async-done(((f32[8,16,512]{2,1,0:T(8,128)}), f32[32,16,512]{2,1,0:T(8,128)}) %all-gather.8.cloned.1.call-update) | async-done | bytes 1048592 | tf_op jit(solution)/shard_map/all_gather | solution.py:15
  277.8 3.4 %while.34 = (s32[]{:T(128)}, f32[8,16]{1,0:T(8,128)S(1)}, f32[8,16]{1,0:T(8,128)S(1)}, f32[8,16,512]{2,1,0:T(8,128)S(1)}, f32[4,8,16]{2,1,0:T(8,128)S(1)}, /*ind...) while((s32[]{:T(128)}, f32[8,16]{1,0:T(8,128)S(1)}, ...), condition=%wide.region_13.14_spmd, body=%wide.region_12.13_spmd.sunk | while | flops 197381 | bytes 791703 | solution.py:21
  281.3 2.6 fusion.28
  (184 shorter events, 51.1 us)
Async XLA Ops:
  6.5 1.6 copy-start
  6.5 3.5 %copy-start.4 = (s32[8,256]{1,0:T(8,128)S(1)}, s32[8,256]{1,0:T(8,128)}, u32[]{:S(2)}) copy-start(s32[8,256]{1,0:T(8,128)} %param.17) | copy-start | bytes 24580
  6.5 3.8 %copy-start.5 = (s32[8]{0:T(128)S(1)}, s32[8]{0:T(128)}, u32[]{:S(2)}) copy-start(s32[8]{0:T(128)} %param.16) | copy-start | bytes 100
  6.5 48.4 %all-gather.6.cloned.1.call-start = ((), (), s32[]{:S(2)}) async-start(), calls=%async_computation.3 | async-start | bytes 1474560 | tf_op jit(solution)/shard_map/all_gather | solution.py:54
  57.6 2.8 copy-start.2
  60.4 0.7 copy-start.1
  66.5 6.3 %copy-start.3 = (pred[8,8,64]{2,1,0:T(8,128)(4,1)S(1)}, pred[8,8,64]{2,1,0:T(8,128)(4,1)}, u32[]{:S(2)}) copy-start(pred[8,8,64]{2,1,0:T(8,128)(4,1)} %copy-done.2) | copy-start | bytes 12292 | tf_op jit(solution)/shard_map/while
  72.7 2.8 copy-start.2
  75.6 0.7 copy-start.1
  82.5 6.9 %copy-start.3 = (pred[8,8,64]{2,1,0:T(8,128)(4,1)S(1)}, pred[8,8,64]{2,1,0:T(8,128)(4,1)}, u32[]{:S(2)}) copy-start(pred[8,8,64]{2,1,0:T(8,128)(4,1)} %copy-done.2) | copy-start | bytes 12292 | tf_op jit(solution)/shard_map/while
  89.4 2.8 copy-start.2
  92.2 0.7 copy-start.1
  99.1 6.9 %copy-start.3 = (pred[8,8,64]{2,1,0:T(8,128)(4,1)S(1)}, pred[8,8,64]{2,1,0:T(8,128)(4,1)}, u32[]{:S(2)}) copy-start(pred[8,8,64]{2,1,0:T(8,128)(4,1)} %copy-done.2) | copy-start | bytes 12292 | tf_op jit(solution)/shard_map/while
  106.0 2.8 copy-start.2
  108.8 0.7 copy-start.1
  115.7 6.9 %copy-start.3 = (pred[8,8,64]{2,1,0:T(8,128)(4,1)S(1)}, pred[8,8,64]{2,1,0:T(8,128)(4,1)}, u32[]{:S(2)}) copy-start(pred[8,8,64]{2,1,0:T(8,128)(4,1)} %copy-done.2) | copy-start | bytes 12292 | tf_op jit(solution)/shard_map/while
  122.6 2.8 copy-start.2
  125.5 0.7 copy-start.1
  132.4 6.9 %copy-start.3 = (pred[8,8,64]{2,1,0:T(8,128)(4,1)S(1)}, pred[8,8,64]{2,1,0:T(8,128)(4,1)}, u32[]{:S(2)}) copy-start(pred[8,8,64]{2,1,0:T(8,128)(4,1)} %copy-done.2) | copy-start | bytes 12292 | tf_op jit(solution)/shard_map/while
  139.3 2.8 copy-start.2
  142.1 0.7 copy-start.1
  149.0 6.9 %copy-start.3 = (pred[8,8,64]{2,1,0:T(8,128)(4,1)S(1)}, pred[8,8,64]{2,1,0:T(8,128)(4,1)}, u32[]{:S(2)}) copy-start(pred[8,8,64]{2,1,0:T(8,128)(4,1)} %copy-done.2) | copy-start | bytes 12292 | tf_op jit(solution)/shard_map/while
  155.9 2.8 copy-start.2
  158.7 0.7 copy-start.1
  165.6 6.9 %copy-start.3 = (pred[8,8,64]{2,1,0:T(8,128)(4,1)S(1)}, pred[8,8,64]{2,1,0:T(8,128)(4,1)}, u32[]{:S(2)}) copy-start(pred[8,8,64]{2,1,0:T(8,128)(4,1)} %copy-done.2) | copy-start | bytes 12292 | tf_op jit(solution)/shard_map/while
  172.5 2.8 copy-start.2
  175.4 0.7 copy-start.1
  182.3 6.9 %copy-start.3 = (pred[8,8,64]{2,1,0:T(8,128)(4,1)S(1)}, pred[8,8,64]{2,1,0:T(8,128)(4,1)}, u32[]{:S(2)}) copy-start(pred[8,8,64]{2,1,0:T(8,128)(4,1)} %copy-done.2) | copy-start | bytes 12292 | tf_op jit(solution)/shard_map/while
  189.9 9.7 %all-to-all-start = ((f32[8,1,128]{2,1,0:T(1,128)}), f32[8,1,128]{2,1,0:T(1,128)S(1)}, u32[]{:S(2)}, u32[]{:S(2)}) async-start(f32[8,1,128]{2,1,0:T(1,128)} %reshape.72), calls=%async_computation | async-start | bytes 8192 | tf_op jit(solution)/shard_map/all_to_all | solution.py:113
  208.4 49.9 %all-to-all-start.2 = ((f32[8,128,512]{2,0,1:T(8,128)}), f32[8,128,512]{2,0,1:T(8,128)}, u32[]{:S(2)}, u32[]{:S(2)}) async-start(f32[8,128,512]{2,0,1:T(8,128)} %get-tuple-element.228), calls=%async_computation.2 | async-start | bytes 4194304 | tf_op jit(solution)/shard_map/all_to_all | solution.py:115
  212.8 64.1 %all-gather.8.cloned.1.call-start = ((), (), s32[]{:S(2)}) async-start(), calls=%async_computation.4 | async-start | bytes 1310720 | tf_op jit(solution)/shard_map/all_gather | solution.py:15
Sparse Core Ops, SparseCore 0:
  10.1 44.7 all-gather.5
  261.1 15.6 all-gather.7
where the time goes:
time: 293 us; the launch traced here: 291 us
  waiting for transfers between devices  89.9 us (31%)
  matrix products  88 us (30%)
  local copies, waits for them, and re-layouts  39.1 us (13%)
  other arithmetic  32.4 us (11%)
  blocking collectives  19.2 us (7%)
  between operations  13.6 us (5%)
  starting transfers between devices  7.69 us (3%)
    dot_general x8, matrix products, body_step(): jnp.einsum('rsh,shc->rhc', weight, slot_latent, precision=lax.Precision.H...  54.4 us
    all_to_all x1, waiting for transfers between devices, local(): lax.all_to_all(partials[2], 'row', split_axis=1, concat_axis=0, tiled=True)  43.4 us
    all_gather x1, waiting for transfers between devices, local(): queries = lax.all_gather(query, 'row', axis=1, tiled=True)  35.8 us
    dot_general x8, matrix products, body_step(): jnp.einsum('sht,stc->shc', expo, key_rows[:, :, :kv_width], preferred_ele...  16.9 us
    unnamed x14, local copies, waits for them, and re-layouts  13.4 us
    add x8, other arithmetic, body_step(): denom = denom * keep + jnp.sum(weight * slot_denom[None, :, :], axis=1)  11.2 us
    all_gather x2, blocking collectives, merged(): everything = jax.tree.map(lambda part: lax.all_gather(part, axis), array)  10.4 us
    dot_general x8, matrix products, body_step(): jnp.einsum('rs,rhd->shd', owner.astype(jnp.bfloat16), queries, preferred_...  9.6 us
  transfers between devices with their start and end apart: 4, of which 4 were waited for; matrix products, arithmetic and copies ran while one was open for 4% of the time, Pallas kernels for 0%

commit v1 on v0

v1 whole, which is shorter than its diff:
```python
import functools

import jax
import jax.numpy as jnp
from jax import lax
from jax.experimental import pallas as pl
from jax.experimental.pallas import tpu as pltpu
from jax.sharding import PartitionSpec as P

HEAD_NOPE_WIDTH = 128
ROTARY_WIDTH = 64
PAGE = 64
GROUP = 4
MASKED = -1e30
MESH = pl.DeviceIdType.MESH
VMEM_LIMIT = 48 * 1024 * 1024


def place(nrh):
    row, col = lax.axis_index("row"), lax.axis_index("col")
    return row // 2, row % 2, col // 4, (col // 2) % 2, col % 2


def device(rh, rl, cg, yl, core):
    return (rh * 2 + rl, cg * 4 + yl * 2 + core)


def greet(peers):
    barrier = pltpu.get_barrier_semaphore()
    for peer in peers:
        pl.semaphore_signal(barrier, inc=1, device_id=peer, device_id_type=MESH)
    pl.semaphore_wait(barrier, len(peers))


def head_diagonal(rows, weights_ref, heads):
    count = rows.shape[0]
    head = lax.broadcasted_iota(jnp.int32, (count, weights_ref.shape[2]), 0) % heads
    total = jnp.zeros((count, weights_ref.shape[2]), jnp.float32)
    for h in range(heads):
        product = jnp.dot(rows, weights_ref[h], preferred_element_type=jnp.float32)
        total = jnp.where(head == h, product, total)
    return total


def gather_kernel(nrh, heads, nope_ref, rope_ref, weights_ref, out_ref, send, recv):
    rh, rl, cg, yl, core = place(nrh)
    q = yl * 2 + core
    qy = (1 - yl) * 2 + core
    z_peer = lambda k: device(k, rl, cg, yl, core)
    x_peer = device(rh, 1 - rl, cg, yl, core)
    y_peer = device(rh, rl, cg, 1 - yl, core)
    c_peer = device(rh, rl, cg, yl, 1 - core)
    greet([z_peer((rh + d) % nrh) for d in range(1, nrh)] + [x_peer, y_peer, c_peer])

    rows = nope_ref[pl.ds(pl.multiple_of(q * 2 * heads, 2 * heads), 2 * heads), :]
    latent = head_diagonal(rows.astype(jnp.bfloat16), weights_ref, heads)
    latent = latent.astype(jnp.bfloat16).astype(out_ref.dtype)
    width = weights_ref.shape[2]
    for i in range(2):
        out_ref[2 * q + i, rl, rh, :, 0:width] = latent[i * heads : (i + 1) * heads]
        out_ref[2 * q + i, rl, rh, :, width:] = rope_ref[2 * q + i]

    started = []

    def copy(a, k, b, slot, peer, send_slot=None):
        shard = out_ref.at[pl.ds(2 * b, 2), a, k]
        return pltpu.make_async_remote_copy(
            src_ref=shard,
            dst_ref=shard,
            send_sem=send.at[slot if send_slot is None else send_slot],
            recv_sem=recv.at[slot],
            device_id=peer,
            device_id_type=MESH,
        )

    def push(*args, **kw):
        one = copy(*args, **kw)
        one.start()
        started.append(one)

    def arrived(a, k, b, slot, peer):
        copy(a, k, b, slot, peer).wait_recv()

    Z, X, Y, D, C = 0, nrh, 2 * nrh, 3 * nrh, 4 * nrh
    half = nrh // 2

    def spread(k):
        push(rl, k, q, X + k, x_peer)
        push(rl, k, q, Y + k, y_peer)
        push(rl, k, q, C + k, c_peer)

    for d in range(1, nrh):
        push(rl, rh, q, Z + rh, z_peer((rh + d) % nrh), send_slot=Z + d)
    spread(rh)
    for d in range(1, nrh):
        k = (rh + d) % nrh
        arrived(rl, k, q, Z + k, z_peer(k))
        spread(k)
    for k in range(nrh):
        arrived(1 - rl, k, q, X + k, x_peer)
        if k >= half:
            push(1 - rl, k, q, D + k, y_peer)
        push(1 - rl, k, q, C + nrh + k, c_peer)
        arrived(rl, k, qy, Y + k, y_peer)
        if k < half:
            push(rl, k, qy, D + k, x_peer)
        push(rl, k, qy, C + 2 * nrh + k, c_peer)
    for k in range(nrh):
        arrived(1 - rl, k, qy, D + k, x_peer if k < half else y_peer)
        push(1 - rl, k, qy, C + 3 * nrh + k, c_peer)
    qc, qyc = yl * 2 + 1 - core, (1 - yl) * 2 + 1 - core
    for k in range(nrh):
        arrived(rl, k, qc, C + k, c_peer)
        arrived(1 - rl, k, qc, C + nrh + k, c_peer)
        arrived(rl, k, qyc, C + 2 * nrh + k, c_peer)
        arrived(1 - rl, k, qyc, C + 3 * nrh + k, c_peer)
    for one in started:
        one.wait_send()


def attend_kernel(
    scale, order_ref, live_ref, first_ref, query_ref, cache_ref, part_ref, stat_ref,
    keys, scores, total, sem,
):
    requests = query_ref.shape[0]
    width = part_ref.shape[2]
    count = first_ref[requests]

    def fetch(k):
        return pltpu.make_async_copy(cache_ref.at[order_ref[k]], keys.at[k], sem.at[k])

    lax.fori_loop(0, count, lambda k, c: (fetch(k).start(), c)[1], 0)
    for i in range(GROUP - 1):
        keys[count + i] = jnp.zeros(keys.shape[1:], keys.dtype)
    lax.fori_loop(0, count, lambda k, c: (fetch(k).wait(), c)[1], 0)

    token = lax.broadcasted_iota(jnp.int32, (PAGE, query_ref.shape[1]), 0)
    line = lax.broadcasted_iota(jnp.int32, stat_ref.shape[1:], 0)
    for r in range(requests):
        begin, end = first_ref[r], first_ref[r + 1]
        groups = (end - begin + GROUP - 1) // GROUP

        def score_step(g, top):
            at = begin + g * GROUP
            rows = keys[pl.ds(at, GROUP)].reshape(GROUP * PAGE, keys.shape[2])
            score = lax.dot_general(
                rows, query_ref[r], (((1,), (1,)), ((), ())), preferred_element_type=jnp.float32
            )
            for j in range(GROUP):
                live = jnp.where(at + j < end, live_ref[at + j], 0)
                piece = jnp.where(token < live, score[j * PAGE : (j + 1) * PAGE] * scale, MASKED)
                scores[g, j * PAGE : (j + 1) * PAGE, :] = piece
                top = jnp.maximum(top, jnp.max(piece, axis=0, keepdims=True))
            return top

        top = lax.fori_loop(
            0, groups, score_step, jnp.full((1, query_ref.shape[1]), MASKED, jnp.float32)
        )
        total[...] = jnp.zeros_like(total)

        def sum_step(g, denom):
            at = begin + g * GROUP
            expo = jnp.exp(scores[g] - top).astype(jnp.bfloat16)
            rows = keys[pl.ds(at, GROUP), :, 0:width].reshape(GROUP * PAGE, width)
            total[...] += lax.dot_general(
                expo, rows, (((0,), (0,)), ((), ())), preferred_element_type=jnp.float32
            )
            return denom + jnp.sum(expo.astype(jnp.float32), axis=0, keepdims=True)

        denom = lax.fori_loop(0, groups, sum_step, jnp.zeros_like(top))
        part_ref[r] = total[...].astype(part_ref.dtype)
        stat_ref[r] = jnp.where(line == 0, top, jnp.where(line == 1, denom, 0.0))


def columns(lines):
    line = lax.broadcasted_iota(jnp.int32, (128, 128), 0)
    table = jnp.zeros((128, 128), jnp.float32)
    for i, one in enumerate(lines):
        table = jnp.where(line == i, one, table)
    return table.T


def reduce_kernel(
    nrh, ncg, heads, part_ref, stat_ref, weights_ref, out_ref,
    core_part, core_stat, y_send, y_stat, y_part, y_stat_in, own, own_stat,
    row_send, row_stat, row_part, row_stat_in, mix, lines, value, send, recv, row_sem_s, row_sem_r,
):
    rh, rl, cg, yl, core = place(nrh)
    nrow = 2 * nrh
    spots = nrow * ncg
    q = yl * 2 + core
    c_peer = device(rh, rl, cg, yl, 1 - core)
    y_peer = device(rh, rl, cg, 1 - yl, core)
    d_peer = device(rh, rl, cg, 1 - yl, 1 - core)
    me = (rl * nrh + rh) * ncg + cg

    def spot(i):
        place_i = i // ncg
        return device(place_i % nrh, place_i // nrh, i % ncg, yl, core)

    barrier = pltpu.get_barrier_semaphore()
    for peer in (c_peer, y_peer, d_peer):
        pl.semaphore_signal(barrier, inc=1, device_id=peer, device_id_type=MESH)

    def hello(d, carry):
        pl.semaphore_signal(
            barrier, inc=1, device_id=spot((me + d) % spots), device_id_type=MESH
        )
        return carry

    lax.fori_loop(1, spots, hello, 0)
    pl.semaphore_wait(barrier, spots + 2)

    def remote(src, dst, slot, peer):
        return pltpu.make_async_remote_copy(
            src_ref=src, dst_ref=dst, send_sem=send.at[slot], recv_sem=recv.at[slot],
            device_id=peer, device_id_type=MESH,
        )

    started = []

    def push(*args):
        one = remote(*args)
        one.start()
        started.append(one)
        return one

    def block_of(y, c):
        return pl.ds(2 * (2 * y + c), 2)

    stat_in = push(stat_ref, core_stat, 0, c_peer)
    core_in = [
        push(part_ref.at[block_of(1 - yl, 1 - core)], core_part.at[0], 1, c_peer),
        push(part_ref.at[block_of(yl, 1 - core)], core_part.at[1], 2, c_peer),
    ]
    line = lax.broadcasted_iota(jnp.int32, (8, 128), 0)

    def merge_stats(first, second):
        top = jnp.maximum(first[0:1], second[0:1])
        one, two = jnp.exp(first[0:1] - top), jnp.exp(second[0:1] - top)
        denom = one * first[1:2] + two * second[1:2]
        return jnp.where(line == 0, top, jnp.where(line == 1, denom, 0.0)), columns((one, two))

    def merge_chunk(i, place_k, first, second):
        weight = mix[i, pl.ds(place_k * heads, heads), :]
        return weight[:, 0:1] * first.astype(jnp.float32) + weight[:, 1:2] * second.astype(
            jnp.float32
        )

    stat_in.wait_recv()
    for side in range(2):
        y = 1 - yl if side == 0 else yl
        stats = y_stat if side == 0 else own_stat
        for i in range(2):
            r = 2 * (2 * y + core) + i
            stats[i], mix[i] = merge_stats(stat_ref[r], core_stat[r])
        if side == 0:
            push(y_stat, y_stat_in, 3, y_peer)
        core_in[side].wait_recv()
        for a in range(2):
            for k in range(nrh):
                for i in range(2):
                    r = 2 * (2 * y + core) + i
                    merged = merge_chunk(
                        i, a * nrh + k, part_ref[r, a, k], core_part[side, i, a, k]
                    )
                    if side == 0:
                        y_send[a, k, i] = merged.astype(y_send.dtype)
                    else:
                        own[a, k, i] = merged
                if side == 0:
                    push(y_send.at[a, k], y_part.at[a, k], 4 + a * nrh + k, y_peer)

    remote(y_stat, y_stat_in, 3, y_peer).wait_recv()
    for i in range(2):
        row_stat[i], mix[i] = merge_stats(own_stat[i], y_stat_in[i])

    def row_copies(to, source, d):
        return (
            pltpu.make_async_remote_copy(
                src_ref=row_send.at[to // ncg], dst_ref=row_part.at[source],
                send_sem=row_sem_s.at[0, d], recv_sem=row_sem_r.at[0, source],
                device_id=spot(to), device_id_type=MESH,
            ),
            pltpu.make_async_remote_copy(
                src_ref=row_stat, dst_ref=row_stat_in.at[source],
                send_sem=row_sem_s.at[1, d], recv_sem=row_sem_r.at[1, source],
                device_id=spot(to), device_id_type=MESH,
            ),
        )

    def send_stat(d, carry):
        row_copies((me + d) % spots, me, d)[1].start()
        return carry

    lax.fori_loop(1, spots, send_stat, 0)
    row_stat_in[me] = row_stat[...]

    def chunk_step(place_k):
        a, k = place_k // nrh, place_k % nrh
        remote(y_send.at[a, k], y_part.at[a, k], 4 + place_k, y_peer).wait_recv()
        for i in range(2):
            row_send[place_k, i] = merge_chunk(
                i, place_k, own[a, k, i], y_part[a, k, i]
            ).astype(row_send.dtype)

    for place_k in range(nrow):
        chunk_step(place_k)

        def send_chunk(g, carry):
            to = place_k * ncg + g

            @pl.when(to != me)
            def _():
                row_copies(to, me, (to - me + spots) % spots)[0].start()

            return carry

        lax.fori_loop(0, ncg, send_chunk, 0)
    row_part[me] = row_send[me // ncg]

    def take_stat(d, carry):
        row_copies(me, (me + d) % spots, d)[1].wait_recv()
        return carry

    lax.fori_loop(1, spots, take_stat, 0)
    my_heads = pl.ds(pl.multiple_of((rl * nrh + rh) * heads, heads), heads)

    def top_step(s, tops):
        new = []
        for i in range(2):
            new.append(jnp.maximum(tops[i], row_stat_in[s, i][0:1]))
        return tuple(new)

    tops = lax.fori_loop(0, spots, top_step, (jnp.full((1, 128), MASKED, jnp.float32),) * 2)

    def denom_step(s, denoms):
        return tuple(
            denoms[i] + jnp.exp(row_stat_in[s, i][0:1] - tops[i]) * row_stat_in[s, i][1:2]
            for i in range(2)
        )

    denoms = lax.fori_loop(0, spots, denom_step, (jnp.zeros((1, 128), jnp.float32),) * 2)
    per = 64
    for i in range(2):
        lines[0, i] = columns((denoms[i],))

    def weight_step(s, carry):
        for i in range(2):
            lines[1 + s, i] = columns((jnp.exp(row_stat_in[s, i][0:1] - tops[i]),))
        return carry

    lax.fori_loop(0, spots, weight_step, 0)

    def take_part(d, carry):
        row_copies(me, (me + d) % spots, d)[0].wait_recv()
        return carry

    lax.fori_loop(1, spots, take_part, 0)

    def sum_step(s, sums):
        return tuple(
            sums[i]
            + lines[1 + s, i, my_heads, :][:, 0:1] * row_part[s, i].astype(jnp.float32)
            for i in range(2)
        )

    width = row_part.shape[-1]
    sums = lax.fori_loop(0, spots, sum_step, (jnp.zeros((heads, width), jnp.float32),) * 2)
    for i in range(2):
        value[i * heads : (i + 1) * heads, :] = sums[i] / lines[0, i, my_heads, :][:, 0:1]
    rows = value[...].astype(jnp.bfloat16)

    out_ref[q] = head_diagonal(rows, weights_ref, heads)
    base = 4 + nrow
    outs = ((c_peer, yl * 2 + 1 - core), (y_peer, (1 - yl) * 2 + core),
            (d_peer, (1 - yl) * 2 + 1 - core))
    for n, (peer, _) in enumerate(outs):
        push(out_ref.at[q], out_ref.at[q], base + n, peer)
    for n, (peer, owner) in enumerate(outs):
        remote(out_ref.at[owner], out_ref.at[owner], base + n, peer).wait_recv()
    for one in started:
        one.wait_send()

    def drain(d, carry):
        for one in row_copies((me + d) % spots, me, d):
            one.wait_send()
        return carry

    lax.fori_loop(1, spots, drain, 0)


def page_lists(page_table, lengths, device_at, slots):
    requests, pages = page_table.shape
    slot = jnp.arange(slots, dtype=jnp.int32)
    page = jnp.arange(pages, dtype=jnp.int32)
    matches = (page_table - device_at * slots)[:, :, None] == slot[None, None, :]
    left = jnp.clip(lengths[:, None] - page[None, :] * PAGE, 0, PAGE)
    live = jnp.sum(jnp.where(matches, left[:, :, None], 0), axis=(0, 1))
    owner = jnp.sum(
        jnp.where(matches, (jnp.arange(requests, dtype=jnp.int32) - requests)[:, None, None], 0),
        axis=(0, 1),
    ) + requests
    ahead = (owner[None, :] < owner[:, None]) | (
        (owner[None, :] == owner[:, None]) & (slot[None, :] < slot[:, None])
    )
    rank = jnp.sum(ahead.astype(jnp.int32), axis=1)
    hit = rank[None, :] == slot[:, None]
    order = jnp.sum(jnp.where(hit, slot[None, :], 0), axis=1)
    live_sorted = jnp.sum(jnp.where(hit, live[None, :], 0), axis=1)
    first = jnp.sum(
        (owner[None, :] < jnp.arange(requests + 1, dtype=jnp.int32)[:, None]).astype(jnp.int32),
        axis=1,
    )
    return order, jnp.pad(live_sorted, (0, GROUP)), first


def local(
    query_nope, query_rope, key_up_weight, value_up_weight, latent_cache, lengths, page_table
):
    scale = float(HEAD_NOPE_WIDTH + ROTARY_WIDTH) ** (-0.5)
    requests, heads, nope = query_nope.shape
    width = key_up_weight.shape[2]
    full = latent_cache.shape[1]
    nrow, ncol = lax.axis_size("row"), lax.axis_size("col")
    nrh, ncg = nrow // 2, ncol // 4
    all_heads = nrow * heads
    slots = latent_cache.shape[0] // PAGE
    wire = jnp.bfloat16 if heads % 16 == 0 else jnp.float32
    vmem = pl.BlockSpec(memory_space=pltpu.VMEM)

    device_at = lax.axis_index("row") * ncol + lax.axis_index("col")
    order, live, first = page_lists(page_table, lengths, device_at, slots)

    queries = pl.pallas_call(
        functools.partial(gather_kernel, nrh, heads),
        out_shape=jax.ShapeDtypeStruct((requests, 2, nrh, heads, full), wire),
        in_specs=[vmem] * 3,
        out_specs=vmem,
        scratch_shapes=[pltpu.SemaphoreType.DMA((8 * nrh,)), pltpu.SemaphoreType.DMA((8 * nrh,))],
        compiler_params=pltpu.CompilerParams(
            collective_id=0, has_side_effects=True, vmem_limit_bytes=VMEM_LIMIT
        ),
        name="gather_queries",
    )(
        query_nope.astype(wire).reshape(requests * heads, nope),
        query_rope.astype(wire),
        key_up_weight,
    )
    queries = queries.reshape(requests, all_heads, full).astype(jnp.bfloat16)

    part, stat = pl.pallas_call(
        functools.partial(attend_kernel, scale),
        out_shape=(
            jax.ShapeDtypeStruct((requests, all_heads, width), wire),
            jax.ShapeDtypeStruct((requests, 8, all_heads), jnp.float32),
        ),
        in_specs=[pl.BlockSpec(memory_space=pltpu.SMEM)] * 3
        + [vmem, pl.BlockSpec(memory_space=pl.ANY)],
        out_specs=(vmem, vmem),
        scratch_shapes=[
            pltpu.VMEM((slots + GROUP, PAGE, full), jnp.bfloat16),
            pltpu.VMEM((slots // GROUP + 1, GROUP * PAGE, all_heads), jnp.float32),
            pltpu.VMEM((all_heads, width), jnp.float32),
            pltpu.SemaphoreType.DMA((slots,)),
        ],
        compiler_params=pltpu.CompilerParams(vmem_limit_bytes=VMEM_LIMIT),
        name="attend_pages",
    )(order, live, first, queries, latent_cache.reshape(slots, PAGE, full))

    spots = nrow * ncg
    f32 = jnp.float32
    shape = (2, nrh, 2, heads, width)
    values = pl.pallas_call(
        functools.partial(reduce_kernel, nrh, ncg, heads),
        out_shape=jax.ShapeDtypeStruct((4, 2 * heads, value_up_weight.shape[2]), f32),
        in_specs=[vmem] * 3,
        out_specs=vmem,
        scratch_shapes=[
            pltpu.VMEM((2, 2, 2, nrh, heads, width), wire),
            pltpu.VMEM((requests, 8, all_heads), f32),
            pltpu.VMEM(shape, wire),
            pltpu.VMEM((2, 8, all_heads), f32),
            pltpu.VMEM(shape, wire),
            pltpu.VMEM((2, 8, all_heads), f32),
            pltpu.VMEM(shape, f32),
            pltpu.VMEM((2, 8, all_heads), f32),
            pltpu.VMEM((nrow, 2, heads, width), wire),
            pltpu.VMEM((2, 8, all_heads), f32),
            pltpu.VMEM((spots, 2, heads, width), wire),
            pltpu.VMEM((spots, 2, 8, all_heads), f32),
            pltpu.VMEM((2, 128, 128), f32),
            pltpu.VMEM((spots + 1, 2, 128, 128), f32),
            pltpu.VMEM((2 * heads, width), f32),
            pltpu.SemaphoreType.DMA((7 + nrow,)),
            pltpu.SemaphoreType.DMA((7 + nrow,)),
            pltpu.SemaphoreType.DMA((2, spots)),
            pltpu.SemaphoreType.DMA((2, spots)),
        ],
        compiler_params=pltpu.CompilerParams(
            collective_id=1, has_side_effects=True, vmem_limit_bytes=VMEM_LIMIT
        ),
        name="reduce_parts",
    )(part.reshape(requests, 2, nrh, heads, width), stat, value_up_weight)
    return values.reshape(requests, heads * value_up_weight.shape[2]).astype(jnp.bfloat16)


def solution(mesh):
    placed = (
        P(None, "row", None),
        P(None, "row", None),
        P("row", None, None),
        P("row", None, None),
        P(("row", "col"), None),
        P(),
        P(),
    )
    return jax.shard_map(
        local, mesh=mesh, in_specs=placed, out_specs=P(None, "row"), check_vma=False
    )
```

time: 293 us -> 61.5 us (0.21)
  waiting for transfers between devices: 89.9 us -> 0 us
  matrix products: 88 us -> 0 us
  Pallas kernels: 0 us -> 47.4 us
  other arithmetic: 32.4 us -> 1.46 us
  local copies, waits for them, and re-layouts: 39.1 us -> 11.4 us
  blocking collectives: 19.2 us -> 0 us
  between operations: 13.6 us -> 0.07 us
  starting transfers between devices: 7.69 us -> 0 us
    dot_general x34 -> x0, matrix products: 88 us -> none  [the longest x8 54.4 us: body_step(): jnp.einsum('rsh,shc->rhc', weight, slot_latent, precision=lax.Precision.H...]
    all_to_all x2 -> x0, waiting for transfers between devices: 48.7 us -> none  [the longest x1 43.4 us: local(): lax.all_to_all(partials[2], 'row', split_axis=1, concat_axis=0, tiled=True)]
    pallas_call x0 -> x3, Pallas kernels: none -> 47.4 us  [the longest x1 19.6 us: local(): pl.pallas_call(functools.partial(reduce_kernel, nrh, ncg, heads), out_sha...]
    all_gather x2 -> x0, waiting for transfers between devices: 41.2 us -> none  [the longest x1 35.8 us: local(): queries = lax.all_gather(query, 'row', axis=1, tiled=True)]
    add x14 -> x1, other arithmetic: 14.4 us -> 0.01 us  [page_lists(): jnp.sum(jnp.where(matches, (jnp.arange(requests, dtype=jnp.int32) - reque...]
    reduce_sum x20 -> x4, other arithmetic: 13.7 us -> 0.65 us  [the longest x1 0.24 us: page_lists(): live = jnp.sum(jnp.where(matches, left[:, :, None], 0), axis=(0, 1))]
    all_gather x2 -> x0, blocking collectives: 10.4 us -> none  [merged(): everything = jax.tree.map(lambda part: lax.all_gather(part, axis), array)]
    squeeze x8 -> x0, local copies, waits for them, and re-layouts: 9.21 us -> none  [local(): lax.scan(body_step, start_carry, (block_keys, block_valid, block_owned))]
  transfers between devices with their start and end apart: 4 -> 0, of which waited for: 4 -> 0; matrix products, arithmetic and copies ran while one was open for 4% -> 0% of each run, Pallas kernels for 0% -> 0%
where the time goes in v1:
time: 61.5 us; the launch traced here: 60.4 us
  Pallas kernels  47.4 us (77%)
  local copies, waits for them, and re-layouts  11.4 us (19%)
  other arithmetic  1.46 us (2%)
    pallas_call x1, Pallas kernels, local(): pl.pallas_call(functools.partial(reduce_kernel, nrh, ncg, heads), out_sha...  19.6 us
    pallas_call x1, Pallas kernels, local(): pl.pallas_call(functools.partial(gather_kernel, nrh, heads), out_shape=ja...  19.3 us
    unnamed x9, local copies, waits for them, and re-layouts  10.8 us
    pallas_call x1, Pallas kernels, local(): pl.pallas_call(functools.partial(attend_kernel, scale), out_shape=(jax.Sh...  8.52 us

profile of v1, /device:TPU:0, one launch (start us, length us, event | category | flops | bytes accessed | tf_op | source)
XLA Modules:
  0.0 60.4 jit_solution(10290568656583804555)
XLA Ops:
  0.0 0.8 %subtract_clamp_fusion = (s32[8,256]{1,0:T(8,128)S(1)}, s32[8,256]{1,0:T(8,128)S(1)}) fusion(s32[256]{0:T(256)S(1)} %iota_multiply_fusion, s32[8]{0:T(128)} %param.12, s32[8,256]{1,0:T(8,128)} %param.13, s32[]{:T(128)S(6)} %mul.18), kind=kLoop, calls=%fused_computation.12 | loop fusion | flops 6144 | bytes 25636 | tf_op jit(solution)/shard_map/jit(clip)/min | solution.py:398
  0.8 0.2 select_reduce_fusion
  1.0 0.1 convert_reduce_fusion.1.first_ref
  1.2 0.2 convert_reduce_fusion
  1.3 0.1 select_reduce_fusion.2
  1.5 0.0 copy-start
  1.5 1.6 %copy-done = bf16[16,128,512]{2,1,0:T(8,128)(2,1)S(1)} copy-done((bf16[16,128,512]{2,1,0:T(8,128)(2,1)S(1)}, bf16[16,128,512]{2,1,0:T(8,128)(2,1)}, u32[]{:S(2)}) %copy-start) | copy-done | bytes 2097176
  3.1 0.0 copy-start.2
  3.1 0.8 %copy-done.2 = bf16[8,16,128]{2,1,0:T(8,128)(2,1)S(1)} copy-done((bf16[8,16,128]{2,1,0:T(8,128)(2,1)S(1)}, bf16[8,16,128]{2,1,0:T(8,128)(2,1)}, u32[]{:S(2)}) %copy-start.2) | copy-done | bytes 32792
  3.8 0.0 copy-start.3
  3.8 0.8 %copy-done.3 = bf16[8,16,64]{2,1,0:T(8,128)(2,1)S(1)} copy-done((bf16[8,16,64]{2,1,0:T(8,128)(2,1)S(1)}, bf16[8,16,64]{2,1,0:T(8,128)(2,1)}, u32[]{:S(2)}) %copy-start.3) | copy-done | bytes 16408
  4.6 19.3 %gather_queries.1 = bf16[8,2,4,16,576]{4,3,2,1,0:T(8,128)(2,1)S(1)} custom-call(bf16[128,128]{1,0:T(8,128)(2,1)S(1)} %bitcast.6, bf16[8,16,64]{2,1,0:T(8,128)(2,1)S(1)} %copy-done.3, bf16[16,128,512]{2,1,0:T(8,128)(2,1)S(1)} %copy-done), custom_call_target="tpu_custom_call" | custom-call | tf_op jit(solution)/shard_map/gather_queries/pallas_call | solution.py:435
  23.9 7.7 %copy.9 = bf16[4096,576]{1,0:T(8,128)(2,1)} copy(bf16[4096,576]{0,1:T(8,128)(2,1)} %param.11) | data formatting | bytes 9437184 | tf_op args[4]
  31.6 0.0 copy-start.1
  31.6 8.5 %attend_pages.1 = (bf16[8,128,512]{2,1,0:T(8,128)(2,1)S(1)}, f32[8,8,128]{2,1,0:T(8,128)S(1)}) custom-call(s32[64]{0:T(128)S(1)} %get-tuple-element.12.order_ref, s32[68]{0:T(128)S(1)} %pad.4.live_ref, s32[9]{0:T(128)S(1)} %convert_reduce_fusion.1.first_ref, bf16[8,128,576]{2,1,0:T(8,128)(2,1)S(1)} %bitcast.4, bf16[64,64,576]{2,1,0:T(8,128)(2,1)} %bitcast.7), custom_call_target="tpu_custom_call" | custom-call | tf_op jit(solution)/shard_map/attend_pages/pallas_call | solution.py:452
  40.1 0.0 copy-done.1
  40.1 19.6 %reduce_parts.1 = f32[4,32,128]{2,1,0:T(8,128)S(1)} custom-call(bf16[8,2,4,16,512]{4,3,2,1,0:T(8,128)(2,1)S(1)} %bitcast.5, f32[8,8,128]{2,1,0:T(8,128)S(1)} %get-tuple-element.8.stat_ref, bf16[16,512,128]{2,1,0:T(8,128)(2,1)S(1)} %copy-done.1), custom_call_target="tpu_custom_call" | custom-call | tf_op jit(solution)/shard_map/reduce_parts/pallas_call | solution.py:474
  59.7 0.6 %convert_element_type.15 = bf16[8,2048]{1,0:T(8,128)(2,1)} reshape(bf16[4,32,128]{2,1,0:T(8,128)(2,1)S(1)} %convert_element_type.14) | data formatting | bytes 65536 | tf_op jit(solution)/shard_map/convert_element_type | solution.py:505
  (5 shorter events, 0.0 us)
Async XLA Ops:
  1.5 1.6 %copy-start = (bf16[16,128,512]{2,1,0:T(8,128)(2,1)S(1)}, bf16[16,128,512]{2,1,0:T(8,128)(2,1)}, u32[]{:S(2)}) copy-start(bf16[16,128,512]{2,1,0:T(8,128)(2,1)} %weights_ref.2) | copy-start | bytes 6291460
  3.1 0.8 %copy-start.2 = (bf16[8,16,128]{2,1,0:T(8,128)(2,1)S(1)}, bf16[8,16,128]{2,1,0:T(8,128)(2,1)}, u32[]{:S(2)}) copy-start(bf16[8,16,128]{2,1,0:T(8,128)(2,1)} %param.7) | copy-start | bytes 98308
  3.8 0.8 %copy-start.3 = (bf16[8,16,64]{2,1,0:T(8,128)(2,1)S(1)}, bf16[8,16,64]{2,1,0:T(8,128)(2,1)}, u32[]{:S(2)}) copy-start(bf16[8,16,64]{2,1,0:T(8,128)(2,1)} %rope_ref.1) | copy-start | bytes 49156
  31.6 8.5 %copy-start.1 = (bf16[16,512,128]{2,1,0:T(8,128)(2,1)S(1)}, bf16[16,512,128]{2,1,0:T(8,128)(2,1)}, u32[]{:S(2)}) copy-start(bf16[16,512,128]{2,1,0:T(8,128)(2,1)} %weights_ref.3) | copy-start | bytes 6291460

commit v2 on v1

--- a/solution.py
+++ b/solution.py
@@ -11,6 +11,9 @@
 ROTARY_WIDTH = 64
 PAGE = 64
 GROUP = 4
+PAIR = 2
+BLOCK = 128
+CACHE_LOADS = 4
 MASKED = -1e30
 MESH = pl.DeviceIdType.MESH
 VMEM_LIMIT = 48 * 1024 * 1024
@@ -42,7 +45,40 @@
     return total
 
 
-def gather_kernel(nrh, heads, nope_ref, rope_ref, weights_ref, out_ref, send, recv):
+def gather_kernel(
+    nrh, heads, nope_hbm, rope_hbm, weights_hbm, cache_hbm, out_ref, keys_ref,
+    nope_ref, rope_ref, weights_ref, cache_ref, local_sem, send, recv,
+):
+    blocks = cache_hbm.shape[1] // BLOCK
+    loads = [
+        pltpu.make_async_copy(nope_hbm, nope_ref, local_sem.at[0]),
+        pltpu.make_async_copy(rope_hbm, rope_ref, local_sem.at[1]),
+        pltpu.make_async_copy(weights_hbm, weights_ref, local_sem.at[2]),
+    ]
+    span = cache_hbm.shape[1] // CACHE_LOADS
+    cache_loads = [
+        pltpu.make_async_copy(
+            cache_hbm.at[:, pl.ds(j * span, span)], cache_ref.at[:, pl.ds(j * span, span)],
+            local_sem.at[3 + j],
+        )
+        for j in range(CACHE_LOADS)
+    ]
+    for one in loads + cache_loads:
+        one.start()
+    turned = [0]
+
+    def turn(count):
+        for _ in range(count):
+            b = turned[0]
+            if b >= blocks:
+                return
+            if b * BLOCK % span == 0:
+                cache_loads[b * BLOCK // span].wait()
+            block = cache_ref[:, b * BLOCK : (b + 1) * BLOCK].T
+            per = BLOCK // PAGE
+            keys_ref[b * per : (b + 1) * per] = block.reshape(per, PAGE, block.shape[1])
+            turned[0] += 1
+
     rh, rl, cg, yl, core = place(nrh)
     q = yl * 2 + core
     qy = (1 - yl) * 2 + core
@@ -52,6 +88,8 @@
     c_peer = device(rh, rl, cg, yl, 1 - core)
     greet([z_peer((rh + d) % nrh) for d in range(1, nrh)] + [x_peer, y_peer, c_peer])
 
+    for one in loads:
+        one.wait()
     rows = nope_ref[pl.ds(pl.multiple_of(q * 2 * heads, 2 * heads), 2 * heads), :]
     latent = head_diagonal(rows.astype(jnp.bfloat16), weights_ref, heads)
     latent = latent.astype(jnp.bfloat16).astype(out_ref.dtype)
@@ -94,9 +132,11 @@
     spread(rh)
     for d in range(1, nrh):
         k = (rh + d) % nrh
+        turn(-(-blocks // (3 * nrh)))
         arrived(rl, k, q, Z + k, z_peer(k))
         spread(k)
     for k in range(nrh):
+        turn(-(-blocks // (3 * nrh)))
         arrived(1 - rl, k, q, X + k, x_peer)
         if k >= half:
             push(1 - rl, k, q, D + k, y_peer)
@@ -106,8 +146,10 @@
             push(rl, k, qy, D + k, x_peer)
         push(rl, k, qy, C + 2 * nrh + k, c_peer)
     for k in range(nrh):
+        turn(-(-blocks // (3 * nrh)))
         arrived(1 - rl, k, qy, D + k, x_peer if k < half else y_peer)
         push(1 - rl, k, qy, C + 3 * nrh + k, c_peer)
+    turn(blocks)
     qc, qyc = yl * 2 + 1 - core, (1 - yl) * 2 + 1 - core
     for k in range(nrh):
         arrived(rl, k, qc, C + k, c_peer)
@@ -119,57 +161,90 @@
 
 
 def attend_kernel(
-    scale, order_ref, live_ref, first_ref, query_ref, cache_ref, part_ref, stat_ref,
-    keys, scores, total, sem,
+    scale, order_ref, live_ref, first_ref, query_ref, keys_ref, part_ref, stat_ref,
+    scores, tops, denoms, total, owner, start,
 ):
-    requests = query_ref.shape[0]
+    requests, heads, _ = query_ref.shape
     width = part_ref.shape[2]
-    count = first_ref[requests]
-
-    def fetch(k):
-        return pltpu.make_async_copy(cache_ref.at[order_ref[k]], keys.at[k], sem.at[k])
-
-    lax.fori_loop(0, count, lambda k, c: (fetch(k).start(), c)[1], 0)
-    for i in range(GROUP - 1):
-        keys[count + i] = jnp.zeros(keys.shape[1:], keys.dtype)
-    lax.fori_loop(0, count, lambda k, c: (fetch(k).wait(), c)[1], 0)
-
-    token = lax.broadcasted_iota(jnp.int32, (PAGE, query_ref.shape[1]), 0)
+
+    def list_request(r, count):
+        begin, end = first_ref[r], first_ref[r + 1]
+        groups = (end - begin + GROUP - 1) // GROUP
+
+        def list_group(g, carry):
+            owner[count + g] = r
+            start[count + g] = begin + g * GROUP
+            return carry
+
+        lax.fori_loop(0, groups, list_group, 0)
+        return count + groups
+
+    count = lax.fori_loop(0, requests, list_request, 0)
+    for i in range(PAIR - 1):
+        owner[count + i] = requests
+        start[count + i] = 0
+    rounds = (count + PAIR - 1) // PAIR
+
+    tops[...] = jnp.full(tops.shape, MASKED, jnp.float32)
+    denoms[...] = jnp.zeros(denoms.shape, jnp.float32)
+    total[...] = jnp.zeros(total.shape, jnp.float32)
+    token = lax.broadcasted_iota(jnp.int32, (PAGE, heads), 0)
+
+    def pages(at, columns_kept):
+        return jnp.concatenate(
+            [keys_ref[order_ref[at + j], :, 0:columns_kept] for j in range(GROUP)], axis=0
+        )
+
+    def score_round(n, carry):
+        products = []
+        for u in range(PAIR):
+            g = n * PAIR + u
+            products.append(
+                lax.dot_general(
+                    pages(start[g], keys_ref.shape[2]),
+                    query_ref[lax.rem(owner[g], requests)],
+                    (((1,), (1,)), ((), ())),
+                    preferred_element_type=jnp.float32,
+                )
+            )
+        for u in range(PAIR):
+            g = n * PAIR + u
+            at, r = start[g], owner[g]
+            end = jnp.where(r < requests, first_ref[jnp.minimum(r, requests - 1) + 1], 0)
+            top = tops[r]
+            for j in range(GROUP):
+                live = jnp.where(at + j < end, live_ref[at + j], 0)
+                rows = slice(j * PAGE, (j + 1) * PAGE)
+                piece = jnp.where(token < live, products[u][rows] * scale, MASKED)
+                scores[g, rows, :] = piece
+                top = jnp.maximum(top, jnp.max(piece, axis=0, keepdims=True))
+            tops[r] = top
+        return carry
+
+    lax.fori_loop(0, rounds, score_round, 0)
+
+    def sum_round(n, carry):
+        products = []
+        for u in range(PAIR):
+            g = n * PAIR + u
+            r = owner[g]
+            expo = jnp.exp(scores[g] - tops[r][0:1]).astype(jnp.bfloat16)
+            denoms[r] += jnp.sum(expo.astype(jnp.float32), axis=0, keepdims=True)
+            products.append(
+                lax.dot_general(
+                    expo, pages(start[g], width), (((0,), (0,)), ((), ())),
+                    preferred_element_type=jnp.float32,
+                )
+            )
+        for u in range(PAIR):
+            total[owner[n * PAIR + u]] += products[u]
+        return carry
+
+    lax.fori_loop(0, rounds, sum_round, 0)
     line = lax.broadcasted_iota(jnp.int32, stat_ref.shape[1:], 0)
     for r in range(requests):
-        begin, end = first_ref[r], first_ref[r + 1]
-        groups = (end - begin + GROUP - 1) // GROUP
-
-        def score_step(g, top):
-            at = begin + g * GROUP
-            rows = keys[pl.ds(at, GROUP)].reshape(GROUP * PAGE, keys.shape[2])
-            score = lax.dot_general(
-                rows, query_ref[r], (((1,), (1,)), ((), ())), preferred_element_type=jnp.float32
-            )
-            for j in range(GROUP):
-                live = jnp.where(at + j < end, live_ref[at + j], 0)
-                piece = jnp.where(token < live, score[j * PAGE : (j + 1) * PAGE] * scale, MASKED)
-                scores[g, j * PAGE : (j + 1) * PAGE, :] = piece
-                top = jnp.maximum(top, jnp.max(piece, axis=0, keepdims=True))
-            return top
-
-        top = lax.fori_loop(
-            0, groups, score_step, jnp.full((1, query_ref.shape[1]), MASKED, jnp.float32)
-        )
-        total[...] = jnp.zeros_like(total)
-
-        def sum_step(g, denom):
-            at = begin + g * GROUP
-            expo = jnp.exp(scores[g] - top).astype(jnp.bfloat16)
-            rows = keys[pl.ds(at, GROUP), :, 0:width].reshape(GROUP * PAGE, width)
-            total[...] += lax.dot_general(
-                expo, rows, (((0,), (0,)), ((), ())), preferred_element_type=jnp.float32
-            )
-            return denom + jnp.sum(expo.astype(jnp.float32), axis=0, keepdims=True)
-
-        denom = lax.fori_loop(0, groups, sum_step, jnp.zeros_like(top))
-        part_ref[r] = total[...].astype(part_ref.dtype)
-        stat_ref[r] = jnp.where(line == 0, top, jnp.where(line == 1, denom, 0.0))
+        part_ref[r] = total[r].astype(part_ref.dtype)
+        stat_ref[r] = jnp.where(line == 0, tops[r], jnp.where(line == 1, denoms[r], 0.0))
 
 
 def columns(lines):
@@ -242,7 +317,7 @@
         return jnp.where(line == 0, top, jnp.where(line == 1, denom, 0.0)), columns((one, two))
 
     def merge_chunk(i, place_k, first, second):
-        weight = mix[i, pl.ds(place_k * heads, heads), :]
+        weight = mix[i, pl.ds(pl.multiple_of(place_k * heads, heads), heads), :]
         return weight[:, 0:1] * first.astype(jnp.float32) + weight[:, 1:2] * second.astype(
             jnp.float32
         )
@@ -257,19 +332,18 @@
         if side == 0:
             push(y_stat, y_stat_in, 3, y_peer)
         core_in[side].wait_recv()
-        for a in range(2):
-            for k in range(nrh):
-                for i in range(2):
-                    r = 2 * (2 * y + core) + i
-                    merged = merge_chunk(
-                        i, a * nrh + k, part_ref[r, a, k], core_part[side, i, a, k]
-                    )
-                    if side == 0:
-                        y_send[a, k, i] = merged.astype(y_send.dtype)
-                    else:
-                        own[a, k, i] = merged
+        for d in range(1, nrow + 1):
+            place_k = (rl * nrh + rh + d) % nrow
+            a, k = place_k // nrh, place_k % nrh
+            for i in range(2):
+                r = 2 * (2 * y + core) + i
+                merged = merge_chunk(i, place_k, part_ref[r, a, k], core_part[side, i, a, k])
                 if side == 0:
-                    push(y_send.at[a, k], y_part.at[a, k], 4 + a * nrh + k, y_peer)
+                    y_send[a, k, i] = merged.astype(y_send.dtype)
+                else:
+                    own[a, k, i] = merged
+            if side == 0:
+                push(y_send.at[a, k], y_part.at[a, k], 3 + d, y_peer)
 
     remote(y_stat, y_stat_in, 3, y_peer).wait_recv()
     for i in range(2):
@@ -296,18 +370,19 @@
     lax.fori_loop(1, spots, send_stat, 0)
     row_stat_in[me] = row_stat[...]
 
-    def chunk_step(place_k):
+    def chunk_step(place_k, d):
         a, k = place_k // nrh, place_k % nrh
-        remote(y_send.at[a, k], y_part.at[a, k], 4 + place_k, y_peer).wait_recv()
+        remote(y_send.at[a, k], y_part.at[a, k], 3 + d, y_peer).wait_recv()
         for i in range(2):
             row_send[place_k, i] = merge_chunk(
                 i, place_k, own[a, k, i], y_part[a, k, i]
             ).astype(row_send.dtype)
 
-    for place_k in range(nrow):
-        chunk_step(place_k)
-
-        def send_chunk(g, carry):
+    for d in range(1, nrow + 1):
+        place_k = (rl * nrh + rh + d) % nrow
+        chunk_step(place_k, d)
+
+        def send_chunk(g, carry, place_k=place_k):
             to = place_k * ncg + g
 
             @pl.when(to != me)
@@ -412,7 +487,7 @@
         (owner[None, :] < jnp.arange(requests + 1, dtype=jnp.int32)[:, None]).astype(jnp.int32),
         axis=1,
     )
-    return order, jnp.pad(live_sorted, (0, GROUP)), first
+    return jnp.pad(order, (0, GROUP)), jnp.pad(live_sorted, (0, GROUP)), first
 
 
 def local(
@@ -432,12 +507,21 @@
     device_at = lax.axis_index("row") * ncol + lax.axis_index("col")
     order, live, first = page_lists(page_table, lengths, device_at, slots)
 
-    queries = pl.pallas_call(
+    queries, keys = pl.pallas_call(
         functools.partial(gather_kernel, nrh, heads),
-        out_shape=jax.ShapeDtypeStruct((requests, 2, nrh, heads, full), wire),
-        in_specs=[vmem] * 3,
-        out_specs=vmem,
-        scratch_shapes=[pltpu.SemaphoreType.DMA((8 * nrh,)), pltpu.SemaphoreType.DMA((8 * nrh,))],
+        out_shape=(
+            jax.ShapeDtypeStruct((requests, 2, nrh, heads, full), wire),
+            jax.ShapeDtypeStruct((slots, PAGE, full), jnp.bfloat16),
+        ),
+        in_specs=[pl.BlockSpec(memory_space=pltpu.HBM)] * 4,
+        out_specs=(vmem, vmem),
+        scratch_shapes=[
+            pltpu.VMEM((requests * heads, nope), wire),
+            pltpu.VMEM(query_rope.shape, wire),
+            pltpu.VMEM(key_up_weight.shape, jnp.bfloat16),
+            pltpu.VMEM((full, slots * PAGE), jnp.bfloat16),
+            pltpu.SemaphoreType.DMA((3 + CACHE_LOADS,)),
+            pltpu.SemaphoreType.DMA((8 * nrh,)), pltpu.SemaphoreType.DMA((8 * nrh,))],
         compiler_params=pltpu.CompilerParams(
             collective_id=0, has_side_effects=True, vmem_limit_bytes=VMEM_LIMIT
         ),
@@ -446,9 +530,11 @@
         query_nope.astype(wire).reshape(requests * heads, nope),
         query_rope.astype(wire),
         key_up_weight,
+        latent_cache.T,
     )
     queries = queries.reshape(requests, all_heads, full).astype(jnp.bfloat16)
 
+    most = slots // GROUP + requests + PAIR
     part, stat = pl.pallas_call(
         functools.partial(attend_kernel, scale),
         out_shape=(
@@ -456,17 +542,19 @@
             jax.ShapeDtypeStruct((requests, 8, all_heads), jnp.float32),
         ),
         in_specs=[pl.BlockSpec(memory_space=pltpu.SMEM)] * 3
-        + [vmem, pl.BlockSpec(memory_space=pl.ANY)],
+        + [vmem, vmem],
         out_specs=(vmem, vmem),
         scratch_shapes=[
-            pltpu.VMEM((slots + GROUP, PAGE, full), jnp.bfloat16),
-            pltpu.VMEM((slots // GROUP + 1, GROUP * PAGE, all_heads), jnp.float32),
-            pltpu.VMEM((all_heads, width), jnp.float32),
-            pltpu.SemaphoreType.DMA((slots,)),
+            pltpu.VMEM((most, GROUP * PAGE, all_heads), jnp.float32),
+            pltpu.VMEM((requests + 1, 8, all_heads), jnp.float32),
+            pltpu.VMEM((requests + 1, 8, all_heads), jnp.float32),
+            pltpu.VMEM((requests + 1, all_heads, width), jnp.float32),
+            pltpu.SMEM((most,), jnp.int32),
+            pltpu.SMEM((most,), jnp.int32),
         ],
         compiler_params=pltpu.CompilerParams(vmem_limit_bytes=VMEM_LIMIT),
         name="attend_pages",
-    )(order, live, first, queries, latent_cache.reshape(slots, PAGE, full))
+    )(order, live, first, queries, keys)
 
     spots = nrow * ncg
     f32 = jnp.float32

time: 61.5 us -> 54.7 us (0.89); the launches traced: 60.4 us -> 54.4 us
  local copies, waits for them, and re-layouts: 11.4 us -> 3.75 us
  Pallas kernels: 47.4 us -> 49.1 us
    unnamed x9 -> x8, local copies, waits for them, and re-layouts: 10.8 us -> 3.11 us
    pallas_call x1, Pallas kernels: 19.3 us -> 22 us  [local(): pl.pallas_call(functools.partial(gather_kernel, nrh, heads), out_shape=(j...]
    pallas_call x1, Pallas kernels: 8.52 us -> 7.57 us  [local(): pl.pallas_call(functools.partial(attend_kernel, scale), out_shape=(jax.Sh...]
where the time goes in v2:
time: 54.7 us; the launch traced here: 54.4 us
  Pallas kernels  49.1 us (90%)
  local copies, waits for them, and re-layouts  3.75 us (7%)
  other arithmetic  1.46 us (3%)
    pallas_call x1, Pallas kernels, local(): pl.pallas_call(functools.partial(gather_kernel, nrh, heads), out_shape=(j...  22 us
    pallas_call x1, Pallas kernels, local(): pl.pallas_call(functools.partial(reduce_kernel, nrh, ncg, heads), out_sha...  19.6 us
    pallas_call x1, Pallas kernels, local(): pl.pallas_call(functools.partial(attend_kernel, scale), out_shape=(jax.Sh...  7.57 us
    unnamed x8, local copies, waits for them, and re-layouts  3.11 us

profile of v2, /device:TPU:0, one launch (start us, length us, event | category | flops | bytes accessed | tf_op | source)
XLA Modules:
  0.0 54.4 jit_solution(1344784491062437827)
XLA Ops:
  0.0 0.8 %subtract_clamp_fusion = (s32[8,256]{1,0:T(8,128)S(1)}, s32[8,256]{1,0:T(8,128)S(1)}) fusion(s32[256]{0:T(256)S(1)} %iota_multiply_fusion, s32[8]{0:T(128)} %param.12, s32[8,256]{1,0:T(8,128)} %param.13, s32[]{:T(128)S(6)} %mul.18), kind=kLoop, calls=%fused_computation.12 | loop fusion | flops 6144 | bytes 25636 | tf_op jit(solution)/shard_map/jit(clip)/min | solution.py:473
  0.8 0.2 select_reduce_fusion
  1.0 0.1 convert_reduce_fusion.1.first_ref
  1.2 0.2 convert_reduce_fusion
  1.3 0.1 select_reduce_fusion.2
  1.5 0.0 copy-start
  1.5 1.6 %copy-done = bf16[16,128,512]{2,1,0:T(8,128)(2,1)S(1)} copy-done((bf16[16,128,512]{2,1,0:T(8,128)(2,1)S(1)}, bf16[16,128,512]{2,1,0:T(8,128)(2,1)}, u32[]{:S(2)}) %copy-start) | copy-done | bytes 2097176
  3.1 0.0 copy-start.2
  3.1 0.8 %copy-done.2 = bf16[8,16,128]{2,1,0:T(8,128)(2,1)S(1)} copy-done((bf16[8,16,128]{2,1,0:T(8,128)(2,1)S(1)}, bf16[8,16,128]{2,1,0:T(8,128)(2,1)}, u32[]{:S(2)}) %copy-start.2) | copy-done | bytes 32792
  3.8 0.0 copy-start.3
  3.8 0.8 %copy-done.3 = bf16[8,16,64]{2,1,0:T(8,128)(2,1)S(1)} copy-done((bf16[8,16,64]{2,1,0:T(8,128)(2,1)S(1)}, bf16[8,16,64]{2,1,0:T(8,128)(2,1)}, u32[]{:S(2)}) %copy-start.3) | copy-done | bytes 16408
  4.6 22.0 %gather_queries.1 = (bf16[8,2,4,16,576]{4,3,2,1,0:T(8,128)(2,1)S(1)}, bf16[64,64,576]{2,1,0:T(8,128)(2,1)}) custom-call(bf16[128,128]{1,0:T(8,128)(2,1)S(1)} %bitcast.6, bf16[8,16,64]{2,1,0:T(8,128)(2,1)S(1)} %copy-done.3, bf16[16,128,512]{2,1,0:T(8,128)(2,1)S(1)} %copy-done, bf16[576,4096]{1,0:T(8,128)(2,1)} %bitcast.7), custom_call_target="tpu_custom_call" | custom-call | tf_op jit(solution)/shard_map/gather_queries/pallas_call | solution.py:510
  26.6 0.0 copy-start.1
  26.6 7.6 %attend_pages.1 = (bf16[8,128,512]{2,1,0:T(8,128)(2,1)S(1)}, f32[8,8,128]{2,1,0:T(8,128)S(1)}) custom-call(s32[68]{0:T(128)S(1)} %pad.7.order_ref, s32[68]{0:T(128)S(1)} %pad.8.live_ref, s32[9]{0:T(128)S(1)} %convert_reduce_fusion.1.first_ref, bf16[8,128,576]{2,1,0:T(8,128)(2,1)S(1)} %bitcast.4, bf16[64,64,576]{2,1,0:T(8,128)(2,1)} %get-tuple-element.10.keys_ref), custom_call_target="tpu_custom_call" | custom-call | tf_op jit(solution)/shard_map/attend_pages/pallas_call | solution.py:538
  34.2 0.0 copy-done.1
  34.2 19.6 %reduce_parts.1 = f32[4,32,128]{2,1,0:T(8,128)S(1)} custom-call(bf16[8,2,4,16,512]{4,3,2,1,0:T(8,128)(2,1)S(1)} %bitcast.5, f32[8,8,128]{2,1,0:T(8,128)S(1)} %get-tuple-element.12.stat_ref, bf16[16,512,128]{2,1,0:T(8,128)(2,1)S(1)} %copy-done.1), custom_call_target="tpu_custom_call" | custom-call | tf_op jit(solution)/shard_map/reduce_parts/pallas_call | solution.py:562
  53.8 0.6 %convert_element_type.15 = bf16[8,2048]{1,0:T(8,128)(2,1)} reshape(bf16[4,32,128]{2,1,0:T(8,128)(2,1)S(1)} %convert_element_type.14) | data formatting | bytes 65536 | tf_op jit(solution)/shard_map/convert_element_type | solution.py:593
  (6 shorter events, 0.0 us)
Async XLA Ops:
  1.5 1.6 %copy-start = (bf16[16,128,512]{2,1,0:T(8,128)(2,1)S(1)}, bf16[16,128,512]{2,1,0:T(8,128)(2,1)}, u32[]{:S(2)}) copy-start(bf16[16,128,512]{2,1,0:T(8,128)(2,1)} %weights_hbm.1) | copy-start | bytes 6291460
  3.1 0.8 %copy-start.2 = (bf16[8,16,128]{2,1,0:T(8,128)(2,1)S(1)}, bf16[8,16,128]{2,1,0:T(8,128)(2,1)}, u32[]{:S(2)}) copy-start(bf16[8,16,128]{2,1,0:T(8,128)(2,1)} %param.7) | copy-start | bytes 98308
  3.8 0.8 %copy-start.3 = (bf16[8,16,64]{2,1,0:T(8,128)(2,1)S(1)}, bf16[8,16,64]{2,1,0:T(8,128)(2,1)}, u32[]{:S(2)}) copy-start(bf16[8,16,64]{2,1,0:T(8,128)(2,1)} %rope_hbm.1) | copy-start | bytes 49156
  26.6 7.6 %copy-start.1 = (bf16[16,512,128]{2,1,0:T(8,128)(2,1)S(1)}, bf16[16,512,128]{2,1,0:T(8,128)(2,1)}, u32[]{:S(2)}) copy-start(bf16[16,512,128]{2,1,0:T(8,128)(2,1)} %weights_ref.1) | copy-start | bytes 6291460

commit v3 on v2

--- a/solution.py
+++ b/solution.py
@@ -14,9 +14,10 @@
 PAIR = 2
 BLOCK = 128
 CACHE_LOADS = 4
+STORED = 4
 MASKED = -1e30
 MESH = pl.DeviceIdType.MESH
-VMEM_LIMIT = 48 * 1024 * 1024
+VMEM_LIMIT = 62 * 1024 * 1024
 
 
 def place(nrh):
@@ -26,13 +27,6 @@
 
 def device(rh, rl, cg, yl, core):
     return (rh * 2 + rl, cg * 4 + yl * 2 + core)
-
-
-def greet(peers):
-    barrier = pltpu.get_barrier_semaphore()
-    for peer in peers:
-        pl.semaphore_signal(barrier, inc=1, device_id=peer, device_id_type=MESH)
-    pl.semaphore_wait(barrier, len(peers))
 
 
 def head_diagonal(rows, weights_ref, heads):
@@ -45,11 +39,64 @@
     return total
 
 
+def list_pages(device_at, slots, length_ref, table_ref, meta_ref):
+    requests, pages = table_ref.shape
+    chunk = 128
+    slot = lax.broadcasted_iota(jnp.int32, (slots, chunk), 0)
+    owner = jnp.zeros((slots, chunk), jnp.int32)
+    live = jnp.zeros((slots, chunk), jnp.int32)
+    for r in range(requests):
+        for c in range(pages // chunk):
+            entry = table_ref[r : r + 1, c * chunk : (c + 1) * chunk] - device_at * slots
+            page = lax.broadcasted_iota(jnp.int32, (1, chunk), 1) + c * chunk
+            left = jnp.clip(length_ref[r] - page * PAGE, 0, PAGE)
+            match = entry == slot
+            owner += jnp.where(match, r - requests, 0)
+            live += jnp.where(match, left, 0)
+    f32 = jnp.float32
+    owner = jnp.sum(owner.astype(f32), axis=1, keepdims=True) + float(requests)
+    live = jnp.sum(live.astype(f32), axis=1, keepdims=True)
+    line = lax.broadcasted_iota(jnp.int32, (128, 128), 0).astype(f32)
+    lane = lax.broadcasted_iota(jnp.int32, (128, 128), 1).astype(f32)
+    spare = 128 - slots
+
+    def fill(column, last):
+        wide = jnp.broadcast_to(column, (slots, 128))
+        return jnp.concatenate([wide, jnp.full((spare, 128), last, f32)], axis=0)
+
+    down = fill(owner, float(requests + 1))
+    across = down.T
+    ahead = (down < across) | ((down == across) & (line < lane))
+    rank = jnp.sum(jnp.where(ahead, 1.0, 0.0), axis=0, keepdims=True)
+    hit = rank == line
+    index = jnp.where(lane < float(slots), lane, 0.0)
+    order = jnp.sum(jnp.where(hit, index, 0.0), axis=1, keepdims=True)
+    sorted_live = jnp.sum(jnp.where(hit, fill(live, 0.0).T, 0.0), axis=1, keepdims=True)
+    first = jnp.sum(jnp.where(down < lane, 1.0, 0.0), axis=0, keepdims=True)
+    both = jnp.where(lane == 0.0, order, jnp.where(lane == 1.0, sorted_live, 0.0)).T
+    rows = jnp.where(line[0:8] == 2.0, first, both[0:8])
+    meta_ref[...] = rows.astype(jnp.int32)
+
+
 def gather_kernel(
-    nrh, heads, nope_hbm, rope_hbm, weights_hbm, cache_hbm, out_ref, keys_ref,
-    nope_ref, rope_ref, weights_ref, cache_ref, local_sem, send, recv,
+    nrh, heads, length_ref, nope_hbm, rope_hbm, weights_hbm, cache_hbm, table_hbm,
+    query_hbm, keys_hbm, meta_ref,
+    nope_ref, rope_ref, weights_ref, cache_ref, table_ref, out_ref, keys_ref,
+    local_sem, store_sem, send, recv,
 ):
+    rh, rl, cg, yl, core = place(nrh)
+    q = yl * 2 + core
+    qy = (1 - yl) * 2 + core
+    z_peer = lambda k: device(k, rl, cg, yl, core)
+    x_peer = device(rh, 1 - rl, cg, yl, core)
+    y_peer = device(rh, rl, cg, 1 - yl, core)
+    c_peer = device(rh, rl, cg, yl, 1 - core)
+    barrier = pltpu.get_barrier_semaphore()
+    peers = [z_peer((rh + d) % nrh) for d in range(1, nrh)] + [x_peer, y_peer, c_peer]
+    for peer in peers:
+        pl.semaphore_signal(barrier, inc=1, device_id=peer, device_id_type=MESH)
     blocks = cache_hbm.shape[1] // BLOCK
+    pages = BLOCK // PAGE
     loads = [
         pltpu.make_async_copy(nope_hbm, nope_ref, local_sem.at[0]),
         pltpu.make_async_copy(rope_hbm, rope_ref, local_sem.at[1]),
@@ -63,8 +110,16 @@
         )
         for j in range(CACHE_LOADS)
     ]
-    for one in loads + cache_loads:
+    load_table = pltpu.make_async_copy(table_hbm, table_ref, local_sem.at[3 + CACHE_LOADS])
+    for one in loads + [load_table] + cache_loads:
         one.start()
+    stores = []
+
+    def store(source, target):
+        one = pltpu.make_async_copy(source, target, store_sem.at[len(stores)])
+        one.start()
+        stores.append(one)
+
     turned = [0]
 
     def turn(count):
@@ -75,18 +130,11 @@
             if b * BLOCK % span == 0:
                 cache_loads[b * BLOCK // span].wait()
             block = cache_ref[:, b * BLOCK : (b + 1) * BLOCK].T
-            per = BLOCK // PAGE
-            keys_ref[b * per : (b + 1) * per] = block.reshape(per, PAGE, block.shape[1])
+            keys_ref[b * pages : (b + 1) * pages] = block.reshape(pages, PAGE, block.shape[1])
             turned[0] += 1
-
-    rh, rl, cg, yl, core = place(nrh)
-    q = yl * 2 + core
-    qy = (1 - yl) * 2 + core
-    z_peer = lambda k: device(k, rl, cg, yl, core)
-    x_peer = device(rh, 1 - rl, cg, yl, core)
-    y_peer = device(rh, rl, cg, 1 - yl, core)
-    c_peer = device(rh, rl, cg, yl, 1 - core)
-    greet([z_peer((rh + d) % nrh) for d in range(1, nrh)] + [x_peer, y_peer, c_peer])
+            if turned[0] % STORED == 0:
+                done = pl.ds((turned[0] - STORED) * pages, STORED * pages)
+                store(keys_ref.at[done], keys_hbm.at[done])
 
     for one in loads:
         one.wait()
@@ -97,6 +145,7 @@
     for i in range(2):
         out_ref[2 * q + i, rl, rh, :, 0:width] = latent[i * heads : (i + 1) * heads]
         out_ref[2 * q + i, rl, rh, :, width:] = rope_ref[2 * q + i]
+    pl.semaphore_wait(barrier, len(peers))
 
     started = []
 
@@ -130,6 +179,9 @@
     for d in range(1, nrh):
         push(rl, rh, q, Z + rh, z_peer((rh + d) % nrh), send_slot=Z + d)
     spread(rh)
+    load_table.wait()
+    device_at = (rh * 2 + rl) * (lax.axis_size("col")) + cg * 4 + q
+    list_pages(device_at, blocks * pages, length_ref, table_ref, meta_ref)
     for d in range(1, nrh):
         k = (rh + d) % nrh
         turn(-(-blocks // (3 * nrh)))
@@ -150,25 +202,57 @@
         arrived(1 - rl, k, qy, D + k, x_peer if k < half else y_peer)
         push(1 - rl, k, qy, C + 3 * nrh + k, c_peer)
     turn(blocks)
+    for b in (q, qy):
+        store(out_ref.at[pl.ds(2 * b, 2)], query_hbm.at[pl.ds(2 * b, 2)])
     qc, qyc = yl * 2 + 1 - core, (1 - yl) * 2 + 1 - core
     for k in range(nrh):
         arrived(rl, k, qc, C + k, c_peer)
         arrived(1 - rl, k, qc, C + nrh + k, c_peer)
         arrived(rl, k, qyc, C + 2 * nrh + k, c_peer)
         arrived(1 - rl, k, qyc, C + 3 * nrh + k, c_peer)
+    for b in (qc, qyc):
+        store(out_ref.at[pl.ds(2 * b, 2)], query_hbm.at[pl.ds(2 * b, 2)])
     for one in started:
         one.wait_send()
+    for one in stores:
+        one.wait()
 
 
 def attend_kernel(
-    scale, order_ref, live_ref, first_ref, query_ref, keys_ref, part_ref, stat_ref,
-    scores, tops, denoms, total, owner, start,
+    scale, meta_ref, query_hbm, keys_hbm, part_hbm, stat_hbm,
+    query_ref, keys_ref, part_ref, stat_ref, scores, tops, denoms, total, owner, start,
+    query_sem, page_sem, out_sem,
 ):
     requests, heads, _ = query_ref.shape
     width = part_ref.shape[2]
+    held = meta_ref[2, requests]
+
+    def fetch(k):
+        return pltpu.make_async_copy(
+            keys_hbm.at[meta_ref[0, k]], keys_ref.at[k], page_sem.at[k]
+        )
+
+    def fetch_query(r):
+        return pltpu.make_async_copy(query_hbm.at[r], query_ref.at[r], query_sem.at[r])
+
+    def start_fetch(k, carry):
+        fetch(k).start()
+        return carry
+
+    def end_fetch(k, carry):
+        fetch(k).wait()
+        return carry
+
+    fetch_query(0).start()
+    lax.fori_loop(0, jnp.minimum(held, 2 * GROUP), start_fetch, 0)
+    for r in range(1, requests):
+        fetch_query(r).start()
+    lax.fori_loop(jnp.minimum(held, 2 * GROUP), held, start_fetch, 0)
+    for i in range(GROUP):
+        keys_ref[held + i] = jnp.zeros(keys_ref.shape[1:], keys_ref.dtype)
 
     def list_request(r, count):
-        begin, end = first_ref[r], first_ref[r + 1]
+        begin, end = meta_ref[2, r], meta_ref[2, r + 1]
         groups = (end - begin + GROUP - 1) // GROUP
 
         def list_group(g, carry):
@@ -191,11 +275,16 @@
     token = lax.broadcasted_iota(jnp.int32, (PAGE, heads), 0)
 
     def pages(at, columns_kept):
-        return jnp.concatenate(
-            [keys_ref[order_ref[at + j], :, 0:columns_kept] for j in range(GROUP)], axis=0
-        )
-
-    def score_round(n, carry):
+        rows = keys_ref[pl.ds(at, GROUP), :, 0:columns_kept]
+        return rows.reshape(GROUP * PAGE, columns_kept)
+
+    for r in range(requests):
+        fetch_query(r).wait()
+
+    def score_round(n, here):
+        need = jnp.maximum(start[n * PAIR], start[n * PAIR + PAIR - 1]) + GROUP
+        need = jnp.maximum(jnp.minimum(need, held), here)
+        lax.fori_loop(here, need, end_fetch, 0)
         products = []
         for u in range(PAIR):
             g = n * PAIR + u
@@ -210,18 +299,19 @@
         for u in range(PAIR):
             g = n * PAIR + u
             at, r = start[g], owner[g]
-            end = jnp.where(r < requests, first_ref[jnp.minimum(r, requests - 1) + 1], 0)
+            end = jnp.where(r < requests, meta_ref[2, jnp.minimum(r, requests - 1) + 1], 0)
             top = tops[r]
             for j in range(GROUP):
-                live = jnp.where(at + j < end, live_ref[at + j], 0)
+                live = jnp.where(at + j < end, meta_ref[1, at + j], 0)
                 rows = slice(j * PAGE, (j + 1) * PAGE)
                 piece = jnp.where(token < live, products[u][rows] * scale, MASKED)
                 scores[g, rows, :] = piece
                 top = jnp.maximum(top, jnp.max(piece, axis=0, keepdims=True))
             tops[r] = top
-        return carry
-
-    lax.fori_loop(0, rounds, score_round, 0)
+        return need
+
+    here = lax.fori_loop(0, rounds, score_round, 0)
+    lax.fori_loop(here, held, end_fetch, 0)
 
     def sum_round(n, carry):
         products = []
@@ -243,8 +333,15 @@
     lax.fori_loop(0, rounds, sum_round, 0)
     line = lax.broadcasted_iota(jnp.int32, stat_ref.shape[1:], 0)
     for r in range(requests):
+        stat_ref[r] = jnp.where(line == 0, tops[r], jnp.where(line == 1, denoms[r], 0.0))
+    outs = [pltpu.make_async_copy(stat_ref, stat_hbm, out_sem.at[requests])]
+    outs[0].start()
+    for r in range(requests):
         part_ref[r] = total[r].astype(part_ref.dtype)
-        stat_ref[r] = jnp.where(line == 0, tops[r], jnp.where(line == 1, denoms[r], 0.0))
+        outs.append(pltpu.make_async_copy(part_ref.at[r], part_hbm.at[r], out_sem.at[r]))
+        outs[-1].start()
+    for one in outs:
+        one.wait()
 
 
 def columns(lines):
@@ -256,8 +353,8 @@
 
 
 def reduce_kernel(
-    nrh, ncg, heads, part_ref, stat_ref, weights_ref, out_ref,
-    core_part, core_stat, y_send, y_stat, y_part, y_stat_in, own, own_stat,
+    nrh, ncg, heads, part_hbm, stat_hbm, weights_hbm, out_ref,
+    part_ref, stat_ref, weights_ref, load_sem, core_part, core_stat, y_send, y_stat, y_part, y_stat_in, own, own_stat,
     row_send, row_stat, row_part, row_stat_in, mix, lines, value, send, recv, row_sem_s, row_sem_r,
 ):
     rh, rl, cg, yl, core = place(nrh)
@@ -284,6 +381,18 @@
         return carry
 
     lax.fori_loop(1, spots, hello, 0)
+
+    def block_of(y, c):
+        return pl.ds(2 * (2 * y + c), 2)
+
+    loads = [
+        pltpu.make_async_copy(stat_hbm, stat_ref, load_sem.at[0]),
+        pltpu.make_async_copy(part_hbm.at[block_of(1 - yl, core)], part_ref.at[0], load_sem.at[1]),
+        pltpu.make_async_copy(part_hbm.at[block_of(yl, core)], part_ref.at[1], load_sem.at[2]),
+        pltpu.make_async_copy(weights_hbm, weights_ref, load_sem.at[3]),
+    ]
+    for one in loads:
+        one.start()
     pl.semaphore_wait(barrier, spots + 2)
 
     def remote(src, dst, slot, peer):
@@ -300,13 +409,10 @@
         started.append(one)
         return one
 
-    def block_of(y, c):
-        return pl.ds(2 * (2 * y + c), 2)
-
-    stat_in = push(stat_ref, core_stat, 0, c_peer)
+    stat_in = push(stat_hbm, core_stat, 0, c_peer)
     core_in = [
-        push(part_ref.at[block_of(1 - yl, 1 - core)], core_part.at[0], 1, c_peer),
-        push(part_ref.at[block_of(yl, 1 - core)], core_part.at[1], 2, c_peer),
+        push(part_hbm.at[block_of(1 - yl, 1 - core)], core_part.at[0], 1, c_peer),
+        push(part_hbm.at[block_of(yl, 1 - core)], core_part.at[1], 2, c_peer),
     ]
     line = lax.broadcasted_iota(jnp.int32, (8, 128), 0)
 
@@ -322,6 +428,8 @@
             jnp.float32
         )
 
+    for one in loads[:3]:
+        one.wait()
     stat_in.wait_recv()
     for side in range(2):
         y = 1 - yl if side == 0 else yl
@@ -336,8 +444,7 @@
             place_k = (rl * nrh + rh + d) % nrow
             a, k = place_k // nrh, place_k % nrh
             for i in range(2):
-                r = 2 * (2 * y + core) + i
-                merged = merge_chunk(i, place_k, part_ref[r, a, k], core_part[side, i, a, k])
+                merged = merge_chunk(i, place_k, part_ref[side, i, a, k], core_part[side, i, a, k])
                 if side == 0:
                     y_send[a, k, i] = merged.astype(y_send.dtype)
                 else:
@@ -378,7 +485,42 @@
                 i, place_k, own[a, k, i], y_part[a, k, i]
             ).astype(row_send.dtype)
 
+    my_heads = pl.ds(pl.multiple_of((rl * nrh + rh) * heads, heads), heads)
+
+    def weigh():
+        def take_stat(d, carry):
+            row_copies(me, (me + d) % spots, d)[1].wait_recv()
+            return carry
+
+        lax.fori_loop(1, spots, take_stat, 0)
+        def top_step(s, tops):
+            new = []
+            for i in range(2):
+                new.append(jnp.maximum(tops[i], row_stat_in[s, i][0:1]))
+            return tuple(new)
+
+        tops = lax.fori_loop(0, spots, top_step, (jnp.full((1, 128), MASKED, jnp.float32),) * 2)
+
+        def denom_step(s, denoms):
+            return tuple(
+                denoms[i] + jnp.exp(row_stat_in[s, i][0:1] - tops[i]) * row_stat_in[s, i][1:2]
+                for i in range(2)
+            )
+
+        denoms = lax.fori_loop(0, spots, denom_step, (jnp.zeros((1, 128), jnp.float32),) * 2)
+        for i in range(2):
+            lines[0, i] = columns((denoms[i],))
+
+        def weight_step(s, carry):
+            for i in range(2):
+                lines[1 + s, i] = columns((jnp.exp(row_stat_in[s, i][0:1] - tops[i]),))
+            return carry
+
+        lax.fori_loop(0, spots, weight_step, 0)
+
     for d in range(1, nrow + 1):
+        if d == max(nrow - 2, 1):
+            weigh()
         place_k = (rl * nrh + rh + d) % nrow
         chunk_step(place_k, d)
 
@@ -393,39 +535,6 @@
 
         lax.fori_loop(0, ncg, send_chunk, 0)
     row_part[me] = row_send[me // ncg]
-
-    def take_stat(d, carry):
-        row_copies(me, (me + d) % spots, d)[1].wait_recv()
-        return carry
-
-    lax.fori_loop(1, spots, take_stat, 0)
-    my_heads = pl.ds(pl.multiple_of((rl * nrh + rh) * heads, heads), heads)
-
-    def top_step(s, tops):
-        new = []
-        for i in range(2):
-            new.append(jnp.maximum(tops[i], row_stat_in[s, i][0:1]))
-        return tuple(new)
-
-    tops = lax.fori_loop(0, spots, top_step, (jnp.full((1, 128), MASKED, jnp.float32),) * 2)
-
-    def denom_step(s, denoms):
-        return tuple(
-            denoms[i] + jnp.exp(row_stat_in[s, i][0:1] - tops[i]) * row_stat_in[s, i][1:2]
-            for i in range(2)
-        )
-
-    denoms = lax.fori_loop(0, spots, denom_step, (jnp.zeros((1, 128), jnp.float32),) * 2)
-    per = 64
-    for i in range(2):
-        lines[0, i] = columns((denoms[i],))
-
-    def weight_step(s, carry):
-        for i in range(2):
-            lines[1 + s, i] = columns((jnp.exp(row_stat_in[s, i][0:1] - tops[i]),))
-        return carry
-
-    lax.fori_loop(0, spots, weight_step, 0)
 
     def take_part(d, carry):
         row_copies(me, (me + d) % spots, d)[0].wait_recv()
@@ -446,6 +555,7 @@
         value[i * heads : (i + 1) * heads, :] = sums[i] / lines[0, i, my_heads, :][:, 0:1]
     rows = value[...].astype(jnp.bfloat16)
 
+    loads[3].wait()
     out_ref[q] = head_diagonal(rows, weights_ref, heads)
     base = 4 + nrow
     outs = ((c_peer, yl * 2 + 1 - core), (y_peer, (1 - yl) * 2 + core),
@@ -463,31 +573,6 @@
         return carry
 
     lax.fori_loop(1, spots, drain, 0)
-
-
-def page_lists(page_table, lengths, device_at, slots):
-    requests, pages = page_table.shape
-    slot = jnp.arange(slots, dtype=jnp.int32)
-    page = jnp.arange(pages, dtype=jnp.int32)
-    matches = (page_table - device_at * slots)[:, :, None] == slot[None, None, :]
-    left = jnp.clip(lengths[:, None] - page[None, :] * PAGE, 0, PAGE)
-    live = jnp.sum(jnp.where(matches, left[:, :, None], 0), axis=(0, 1))
-    owner = jnp.sum(
-        jnp.where(matches, (jnp.arange(requests, dtype=jnp.int32) - requests)[:, None, None], 0),
-        axis=(0, 1),
-    ) + requests
-    ahead = (owner[None, :] < owner[:, None]) | (
-        (owner[None, :] == owner[:, None]) & (slot[None, :] < slot[:, None])
-    )
-    rank = jnp.sum(ahead.astype(jnp.int32), axis=1)
-    hit = rank[None, :] == slot[:, None]
-    order = jnp.sum(jnp.where(hit, slot[None, :], 0), axis=1)
-    live_sorted = jnp.sum(jnp.where(hit, live[None, :], 0), axis=1)
-    first = jnp.sum(
-        (owner[None, :] < jnp.arange(requests + 1, dtype=jnp.int32)[:, None]).astype(jnp.int32),
-        axis=1,
-    )
-    return jnp.pad(order, (0, GROUP)), jnp.pad(live_sorted, (0, GROUP)), first
 
 
 def local(
@@ -503,34 +588,40 @@
     slots = latent_cache.shape[0] // PAGE
     wire = jnp.bfloat16 if heads % 16 == 0 else jnp.float32
     vmem = pl.BlockSpec(memory_space=pltpu.VMEM)
-
-    device_at = lax.axis_index("row") * ncol + lax.axis_index("col")
-    order, live, first = page_lists(page_table, lengths, device_at, slots)
-
-    queries, keys = pl.pallas_call(
+    smem = pl.BlockSpec(memory_space=pltpu.SMEM)
+    hbm = pl.BlockSpec(memory_space=pl.ANY)
+
+    queries, keys, meta = pl.pallas_call(
         functools.partial(gather_kernel, nrh, heads),
         out_shape=(
             jax.ShapeDtypeStruct((requests, 2, nrh, heads, full), wire),
             jax.ShapeDtypeStruct((slots, PAGE, full), jnp.bfloat16),
+            jax.ShapeDtypeStruct((8, 128), jnp.int32),
         ),
-        in_specs=[pl.BlockSpec(memory_space=pltpu.HBM)] * 4,
-        out_specs=(vmem, vmem),
+        in_specs=[smem] + [hbm] * 5,
+        out_specs=(hbm, hbm, vmem),
         scratch_shapes=[
             pltpu.VMEM((requests * heads, nope), wire),
             pltpu.VMEM(query_rope.shape, wire),
             pltpu.VMEM(key_up_weight.shape, jnp.bfloat16),
             pltpu.VMEM((full, slots * PAGE), jnp.bfloat16),
-            pltpu.SemaphoreType.DMA((3 + CACHE_LOADS,)),
+            pltpu.VMEM(page_table.shape, jnp.int32),
+            pltpu.VMEM((requests, 2, nrh, heads, full), wire),
+            pltpu.VMEM((slots, PAGE, full), jnp.bfloat16),
+            pltpu.SemaphoreType.DMA((4 + CACHE_LOADS,)),
+            pltpu.SemaphoreType.DMA((4 + slots * PAGE // (BLOCK * STORED),)),
             pltpu.SemaphoreType.DMA((8 * nrh,)), pltpu.SemaphoreType.DMA((8 * nrh,))],
         compiler_params=pltpu.CompilerParams(
             collective_id=0, has_side_effects=True, vmem_limit_bytes=VMEM_LIMIT
         ),
         name="gather_queries",
     )(
+        lengths,
         query_nope.astype(wire).reshape(requests * heads, nope),
         query_rope.astype(wire),
         key_up_weight,
         latent_cache.T,
+        page_table,
     )
     queries = queries.reshape(requests, all_heads, full).astype(jnp.bfloat16)
 
@@ -541,20 +632,26 @@
             jax.ShapeDtypeStruct((requests, all_heads, width), wire),
             jax.ShapeDtypeStruct((requests, 8, all_heads), jnp.float32),
         ),
-        in_specs=[pl.BlockSpec(memory_space=pltpu.SMEM)] * 3
-        + [vmem, vmem],
-        out_specs=(vmem, vmem),
+        in_specs=[smem, hbm, hbm],
+        out_specs=(hbm, hbm),
         scratch_shapes=[
+            pltpu.VMEM((requests, all_heads, full), jnp.bfloat16),
+            pltpu.VMEM((slots + GROUP, PAGE, full), jnp.bfloat16),
+            pltpu.VMEM((requests, all_heads, width), wire),
+            pltpu.VMEM((requests, 8, all_heads), jnp.float32),
             pltpu.VMEM((most, GROUP * PAGE, all_heads), jnp.float32),
             pltpu.VMEM((requests + 1, 8, all_heads), jnp.float32),
             pltpu.VMEM((requests + 1, 8, all_heads), jnp.float32),
             pltpu.VMEM((requests + 1, all_heads, width), jnp.float32),
             pltpu.SMEM((most,), jnp.int32),
             pltpu.SMEM((most,), jnp.int32),
+            pltpu.SemaphoreType.DMA((requests,)),
+            pltpu.SemaphoreType.DMA((slots,)),
+            pltpu.SemaphoreType.DMA((requests + 1,)),
         ],
         compiler_params=pltpu.CompilerParams(vmem_limit_bytes=VMEM_LIMIT),
         name="attend_pages",
-    )(order, live, first, queries, keys)
+    )(meta, queries, keys)
 
     spots = nrow * ncg
     f32 = jnp.float32
@@ -562,9 +659,13 @@
     values = pl.pallas_call(
         functools.partial(reduce_kernel, nrh, ncg, heads),
         out_shape=jax.ShapeDtypeStruct((4, 2 * heads, value_up_weight.shape[2]), f32),
-        in_specs=[vmem] * 3,
+        in_specs=[hbm] * 3,
         out_specs=vmem,
         scratch_shapes=[
+            pltpu.VMEM((2, 2, 2, nrh, heads, width), wire),
+            pltpu.VMEM((requests, 8, all_heads), f32),
+            pltpu.VMEM(value_up_weight.shape, jnp.bfloat16),
+            pltpu.SemaphoreType.DMA((4,)),
             pltpu.VMEM((2, 2, 2, nrh, heads, width), wire),
             pltpu.VMEM((requests, 8, all_heads), f32),
             pltpu.VMEM(shape, wire),

time: 54.7 us -> 52.8 us (0.965)
  local copies, waits for them, and re-layouts: 3.75 us -> 0.63 us
  Pallas kernels: 49.1 us -> 50.8 us
  other arithmetic: 1.46 us -> 0.85 us
    pallas_call x1, Pallas kernels: 19.6 us -> 23.6 us  [local(): pl.pallas_call(functools.partial(reduce_kernel, nrh, ncg, heads), out_sha...]
    unnamed x8 -> x0, local copies, waits for them, and re-layouts: 3.11 us -> none
    pallas_call x1, Pallas kernels: 22 us -> 19.9 us  [local(): pl.pallas_call(functools.partial(gather_kernel, nrh, heads), out_shape=(j...]
    convert_element_type x1, other arithmetic: 0.01 us -> 0.85 us  [local(): values.reshape(requests, heads * value_up_weight.shape[2])]
    min x1 -> x0, other arithmetic: 0.79 us -> none  [page_lists(): left = jnp.clip(lengths[:, None] - page[None, :] * PAGE, 0, PAGE)]
    reduce_sum x4 -> x0, other arithmetic: 0.65 us -> none  [the longest x1 0.24 us: page_lists(): live = jnp.sum(jnp.where(matches, left[:, :, None], 0), axis=(0, 1))]
where the time goes in v3:
time: 52.8 us; the launch traced here: 52.3 us
  Pallas kernels  50.8 us (96%)
  other arithmetic  0.85 us (2%)
  local copies, waits for them, and re-layouts  0.63 us (1%)
    pallas_call x1, Pallas kernels, local(): pl.pallas_call(functools.partial(reduce_kernel, nrh, ncg, heads), out_sha...  23.6 us
    pallas_call x1, Pallas kernels, local(): pl.pallas_call(functools.partial(gather_kernel, nrh, heads), out_shape=(j...  19.9 us
    pallas_call x1, Pallas kernels, local(): pl.pallas_call(functools.partial(attend_kernel, scale), out_shape=(jax.Sh...  7.24 us

profile of v3, /device:TPU:0, one launch (start us, length us, event | category | flops | bytes accessed | tf_op | source)
XLA Modules:
  0.0 52.3 jit_solution(4750309482404007348)
XLA Ops:
  0.0 19.9 %gather_queries.1 = (bf16[8,2,4,16,576]{4,3,2,1,0:T(8,128)(2,1)}, bf16[64,64,576]{2,1,0:T(8,128)(2,1)}, s32[8,128]{1,0:T(8,128)}) custom-call(s32[8]{0:T(128)} %length_ref.1, bf16[128,128]{1,0:T(8,128)(2,1)} %bitcast.7, bf16[8,16,64]{2,1,0:T(8,128)(2,1)} %rope_hbm.1, bf16[16,128,512]{2,1,0:T(8,128)(2,1)} %weights_hbm.2, bf16[576,4096]{1,0:T(8,128)(2,1)} %bitcast.4, ...), custom_call_target="tpu_custom_call" | custom-call | tf_op jit(solution)/shard_map/gather_queries/pallas_call | solution.py:594
  19.9 7.2 %attend_pages.1 = (bf16[8,128,512]{2,1,0:T(8,128)(2,1)}, f32[8,8,128]{2,1,0:T(8,128)}) custom-call(s32[8,128]{1,0:T(8,128)} %get-tuple-element.10.meta_ref, bf16[8,128,576]{2,1,0:T(8,128)(2,1)} %bitcast.5, bf16[64,64,576]{2,1,0:T(8,128)(2,1)} %get-tuple-element.12.keys_hbm), custom_call_target="tpu_custom_call" | custom-call | tf_op jit(solution)/shard_map/attend_pages/pallas_call | solution.py:629
  27.2 23.6 %reduce_parts.1 = f32[4,32,128]{2,1,0:T(8,128)} custom-call(bf16[8,2,4,16,512]{4,3,2,1,0:T(8,128)(2,1)} %bitcast.6, f32[8,8,128]{2,1,0:T(8,128)} %get-tuple-element.14.stat_hbm, bf16[16,512,128]{2,1,0:T(8,128)(2,1)} %weights_hbm.3), custom_call_target="tpu_custom_call" | custom-call | tf_op jit(solution)/shard_map/reduce_parts/pallas_call | solution.py:659
  50.8 0.8 %convert_element_type.6 = bf16[4,32,128]{2,1,0:T(8,128)(2,1)S(1)} convert(f32[4,32,128]{2,1,0:T(8,128)} %reduce_parts.1) | non-fusion elementwise | flops 16384 | bytes 98304 | tf_op jit(solution)/shard_map/convert_element_type | solution.py:694
  51.6 0.6 %convert_element_type.7 = bf16[8,2048]{1,0:T(8,128)(2,1)} reshape(bf16[4,32,128]{2,1,0:T(8,128)(2,1)S(1)} %convert_element_type.6) | data formatting | bytes 65536 | tf_op jit(solution)/shard_map/convert_element_type | solution.py:694

commit v4 on v3

--- a/solution.py
+++ b/solution.py
@@ -111,7 +111,7 @@
         for j in range(CACHE_LOADS)
     ]
     load_table = pltpu.make_async_copy(table_hbm, table_ref, local_sem.at[3 + CACHE_LOADS])
-    for one in loads + [load_table] + cache_loads:
+    for one in loads + [load_table]:
         one.start()
     stores = []
 
@@ -138,6 +138,8 @@
 
     for one in loads:
         one.wait()
+    for one in cache_loads:
+        one.start()
     rows = nope_ref[pl.ds(pl.multiple_of(q * 2 * heads, 2 * heads), 2 * heads), :]
     latent = head_diagonal(rows.astype(jnp.bfloat16), weights_ref, heads)
     latent = latent.astype(jnp.bfloat16).astype(out_ref.dtype)
@@ -219,9 +221,8 @@
 
 
 def attend_kernel(
-    scale, meta_ref, query_hbm, keys_hbm, part_hbm, stat_hbm,
-    query_ref, keys_ref, part_ref, stat_ref, scores, tops, denoms, total, owner, start,
-    query_sem, page_sem, out_sem,
+    scale, meta_ref, query_hbm, keys_hbm, part_ref, stat_ref,
+    query_ref, keys_ref, scores, tops, denoms, total, owner, start, query_sem, page_sem,
 ):
     requests, heads, _ = query_ref.shape
     width = part_ref.shape[2]
@@ -334,14 +335,7 @@
     line = lax.broadcasted_iota(jnp.int32, stat_ref.shape[1:], 0)
     for r in range(requests):
         stat_ref[r] = jnp.where(line == 0, tops[r], jnp.where(line == 1, denoms[r], 0.0))
-    outs = [pltpu.make_async_copy(stat_ref, stat_hbm, out_sem.at[requests])]
-    outs[0].start()
-    for r in range(requests):
         part_ref[r] = total[r].astype(part_ref.dtype)
-        outs.append(pltpu.make_async_copy(part_ref.at[r], part_hbm.at[r], out_sem.at[r]))
-        outs[-1].start()
-    for one in outs:
-        one.wait()
 
 
 def columns(lines):
@@ -353,8 +347,7 @@
 
 
 def reduce_kernel(
-    nrh, ncg, heads, part_hbm, stat_hbm, weights_hbm, out_ref,
-    part_ref, stat_ref, weights_ref, load_sem, core_part, core_stat, y_send, y_stat, y_part, y_stat_in, own, own_stat,
+    nrh, ncg, heads, part_ref, stat_ref, weights_ref, out_ref, shared, core_part, core_stat, y_send, y_stat, y_part, y_stat_in, own, own_stat,
     row_send, row_stat, row_part, row_stat_in, mix, lines, value, send, recv, row_sem_s, row_sem_r,
 ):
     rh, rl, cg, yl, core = place(nrh)
@@ -385,14 +378,6 @@
     def block_of(y, c):
         return pl.ds(2 * (2 * y + c), 2)
 
-    loads = [
-        pltpu.make_async_copy(stat_hbm, stat_ref, load_sem.at[0]),
-        pltpu.make_async_copy(part_hbm.at[block_of(1 - yl, core)], part_ref.at[0], load_sem.at[1]),
-        pltpu.make_async_copy(part_hbm.at[block_of(yl, core)], part_ref.at[1], load_sem.at[2]),
-        pltpu.make_async_copy(weights_hbm, weights_ref, load_sem.at[3]),
-    ]
-    for one in loads:
-        one.start()
     pl.semaphore_wait(barrier, spots + 2)
 
     def remote(src, dst, slot, peer):
@@ -409,11 +394,19 @@
         started.append(one)
         return one
 
-    stat_in = push(stat_hbm, core_stat, 0, c_peer)
-    core_in = [
-        push(part_hbm.at[block_of(1 - yl, 1 - core)], core_part.at[0], 1, c_peer),
-        push(part_hbm.at[block_of(yl, 1 - core)], core_part.at[1], 2, c_peer),
-    ]
+    stat_in = push(stat_ref, core_stat, 0, c_peer)
+    base = 4 + nrow
+    core_in = []
+    for d in range(1, nrow + 1):
+        place_k = (rl * nrh + rh + d) % nrow
+        a, k = place_k // nrh, place_k % nrh
+        core_in.append(
+            push(
+                part_ref.at[block_of(1 - yl, 1 - core), a, k], core_part.at[0, :, a, k],
+                base + 2 + d, c_peer,
+            )
+        )
+    own_in = push(part_ref.at[block_of(yl, 1 - core)], core_part.at[1], 2, c_peer)
     line = lax.broadcasted_iota(jnp.int32, (8, 128), 0)
 
     def merge_stats(first, second):
@@ -428,8 +421,6 @@
             jnp.float32
         )
 
-    for one in loads[:3]:
-        one.wait()
     stat_in.wait_recv()
     for side in range(2):
         y = 1 - yl if side == 0 else yl
@@ -439,12 +430,16 @@
             stats[i], mix[i] = merge_stats(stat_ref[r], core_stat[r])
         if side == 0:
             push(y_stat, y_stat_in, 3, y_peer)
-        core_in[side].wait_recv()
+        if side == 1:
+            own_in.wait_recv()
         for d in range(1, nrow + 1):
             place_k = (rl * nrh + rh + d) % nrow
             a, k = place_k // nrh, place_k % nrh
+            if side == 0:
+                core_in[d - 1].wait_recv()
             for i in range(2):
-                merged = merge_chunk(i, place_k, part_ref[side, i, a, k], core_part[side, i, a, k])
+                r = 2 * (2 * y + core) + i
+                merged = merge_chunk(i, place_k, part_ref[r, a, k], core_part[side, i, a, k])
                 if side == 0:
                     y_send[a, k, i] = merged.astype(y_send.dtype)
                 else:
@@ -519,8 +514,6 @@
         lax.fori_loop(0, spots, weight_step, 0)
 
     for d in range(1, nrow + 1):
-        if d == max(nrow - 2, 1):
-            weigh()
         place_k = (rl * nrh + rh + d) % nrow
         chunk_step(place_k, d)
 
@@ -535,6 +528,8 @@
 
         lax.fori_loop(0, ncg, send_chunk, 0)
     row_part[me] = row_send[me // ncg]
+
+    weigh()
 
     def take_part(d, carry):
         row_copies(me, (me + d) % spots, d)[0].wait_recv()
@@ -555,15 +550,17 @@
         value[i * heads : (i + 1) * heads, :] = sums[i] / lines[0, i, my_heads, :][:, 0:1]
     rows = value[...].astype(jnp.bfloat16)
 
-    loads[3].wait()
-    out_ref[q] = head_diagonal(rows, weights_ref, heads)
-    base = 4 + nrow
+    shared[q] = head_diagonal(rows, weights_ref, heads).reshape(2, heads, shared.shape[3])
     outs = ((c_peer, yl * 2 + 1 - core), (y_peer, (1 - yl) * 2 + core),
             (d_peer, (1 - yl) * 2 + 1 - core))
     for n, (peer, _) in enumerate(outs):
-        push(out_ref.at[q], out_ref.at[q], base + n, peer)
+        push(shared.at[q], shared.at[q], base + n, peer)
     for n, (peer, owner) in enumerate(outs):
-        remote(out_ref.at[owner], out_ref.at[owner], base + n, peer).wait_recv()
+        remote(shared.at[owner], shared.at[owner], base + n, peer).wait_recv()
+    size = shared.shape[3]
+    for h in range(heads):
+        block = shared[:, :, h, :].reshape(8, size)
+        out_ref[:, h * size : (h + 1) * size] = block.astype(out_ref.dtype)
     for one in started:
         one.wait_send()
 
@@ -633,12 +630,10 @@
             jax.ShapeDtypeStruct((requests, 8, all_heads), jnp.float32),
         ),
         in_specs=[smem, hbm, hbm],
-        out_specs=(hbm, hbm),
+        out_specs=(vmem, vmem),
         scratch_shapes=[
             pltpu.VMEM((requests, all_heads, full), jnp.bfloat16),
             pltpu.VMEM((slots + GROUP, PAGE, full), jnp.bfloat16),
-            pltpu.VMEM((requests, all_heads, width), wire),
-            pltpu.VMEM((requests, 8, all_heads), jnp.float32),
             pltpu.VMEM((most, GROUP * PAGE, all_heads), jnp.float32),
             pltpu.VMEM((requests + 1, 8, all_heads), jnp.float32),
             pltpu.VMEM((requests + 1, 8, all_heads), jnp.float32),
@@ -647,9 +642,8 @@
             pltpu.SMEM((most,), jnp.int32),
             pltpu.SemaphoreType.DMA((requests,)),
             pltpu.SemaphoreType.DMA((slots,)),
-            pltpu.SemaphoreType.DMA((requests + 1,)),
         ],
-        compiler_params=pltpu.CompilerParams(vmem_limit_bytes=VMEM_LIMIT),
+        compiler_params=pltpu.CompilerParams(vmem_limit_bytes=52 * 1024 * 1024),
         name="attend_pages",
     )(meta, queries, keys)
 
@@ -658,14 +652,13 @@
     shape = (2, nrh, 2, heads, width)
     values = pl.pallas_call(
         functools.partial(reduce_kernel, nrh, ncg, heads),
-        out_shape=jax.ShapeDtypeStruct((4, 2 * heads, value_up_weight.shape[2]), f32),
-        in_specs=[hbm] * 3,
+        out_shape=jax.ShapeDtypeStruct(
+            (requests, heads * value_up_weight.shape[2]), jnp.bfloat16
+        ),
+        in_specs=[vmem] * 3,
         out_specs=vmem,
         scratch_shapes=[
-            pltpu.VMEM((2, 2, 2, nrh, heads, width), wire),
-            pltpu.VMEM((requests, 8, all_heads), f32),
-            pltpu.VMEM(value_up_weight.shape, jnp.bfloat16),
-            pltpu.SemaphoreType.DMA((4,)),
+            pltpu.VMEM((4, 2, heads, value_up_weight.shape[2]), f32),
             pltpu.VMEM((2, 2, 2, nrh, heads, width), wire),
             pltpu.VMEM((requests, 8, all_heads), f32),
             pltpu.VMEM(shape, wire),
@@ -681,17 +674,17 @@
             pltpu.VMEM((2, 128, 128), f32),
             pltpu.VMEM((spots + 1, 2, 128, 128), f32),
             pltpu.VMEM((2 * heads, width), f32),
-            pltpu.SemaphoreType.DMA((7 + nrow,)),
-            pltpu.SemaphoreType.DMA((7 + nrow,)),
+            pltpu.SemaphoreType.DMA((7 + 2 * nrow,)),
+            pltpu.SemaphoreType.DMA((7 + 2 * nrow,)),
             pltpu.SemaphoreType.DMA((2, spots)),
             pltpu.SemaphoreType.DMA((2, spots)),
         ],
         compiler_params=pltpu.CompilerParams(
-            collective_id=1, has_side_effects=True, vmem_limit_bytes=VMEM_LIMIT
+            collective_id=1, has_side_effects=True, vmem_limit_bytes=40 * 1024 * 1024
         ),
         name="reduce_parts",
     )(part.reshape(requests, 2, nrh, heads, width), stat, value_up_weight)
-    return values.reshape(requests, heads * value_up_weight.shape[2]).astype(jnp.bfloat16)
+    return values
 
 
 def solution(mesh):

time: 52.8 us -> 50.2 us (0.951)
  Pallas kernels: 50.8 us -> 48.8 us
  other arithmetic: 0.85 us -> 0 us
  local copies, waits for them, and re-layouts: 0.63 us -> 1.29 us
    pallas_call x1, Pallas kernels: 23.6 us -> 21.9 us  [local(): pl.pallas_call(functools.partial(reduce_kernel, nrh, ncg, heads), out_sha...]
    unnamed x0 -> x5, local copies, waits for them, and re-layouts: none -> 1.29 us
    convert_element_type x1 -> x0, other arithmetic: 0.85 us -> none  [local(): values.reshape(requests, heads * value_up_weight.shape[2])]
    convert_element_type x1 -> x0, local copies, waits for them, and re-layouts: 0.63 us -> none  [local(): values.reshape(requests, heads * value_up_weight.shape[2])]
where the time goes in v4:
time: 50.2 us; the launch traced here: 50.1 us
  Pallas kernels  48.8 us (97%)
  local copies, waits for them, and re-layouts  1.29 us (3%)
    pallas_call x1, Pallas kernels, local(): pl.pallas_call(functools.partial(reduce_kernel, nrh, ncg, heads), out_sha...  21.9 us
    pallas_call x1, Pallas kernels, local(): pl.pallas_call(functools.partial(gather_kernel, nrh, heads), out_shape=(j...  19.9 us
    pallas_call x1, Pallas kernels, local(): pl.pallas_call(functools.partial(attend_kernel, scale), out_shape=(jax.Sh...  6.93 us
    unnamed x5, local copies, waits for them, and re-layouts  1.29 us

profile of v4, /device:TPU:0, one launch (start us, length us, event | category | flops | bytes accessed | tf_op | source)
XLA Modules:
  0.0 50.1 jit_solution(1516739577526862349)
XLA Ops:
  0.0 19.9 %gather_queries.1 = (bf16[8,2,4,16,576]{4,3,2,1,0:T(8,128)(2,1)}, bf16[64,64,576]{2,1,0:T(8,128)(2,1)}, s32[8,128]{1,0:T(8,128)}) custom-call(s32[8]{0:T(128)} %length_ref.1, bf16[128,128]{1,0:T(8,128)(2,1)} %bitcast.7, bf16[8,16,64]{2,1,0:T(8,128)(2,1)} %rope_hbm.1, bf16[16,128,512]{2,1,0:T(8,128)(2,1)} %weights_hbm.1, bf16[576,4096]{1,0:T(8,128)(2,1)} %bitcast.5, ...), custom_call_target="tpu_custom_call" | custom-call | tf_op jit(solution)/shard_map/gather_queries/pallas_call | solution.py:591
  19.9 0.0 copy-start.1
  19.9 0.7 %copy-done.1 = s32[8,128]{1,0:T(8,128)S(1)} copy-done((s32[8,128]{1,0:T(8,128)S(1)}, s32[8,128]{1,0:T(8,128)}, u32[]{:S(2)}) %copy-start.1) | copy-done | bytes 4120
  20.6 0.0 copy-start
  20.6 6.9 %attend_pages.1 = (bf16[8,128,512]{2,1,0:T(8,128)(2,1)S(1)}, f32[8,8,128]{2,1,0:T(8,128)S(1)}) custom-call(s32[8,128]{1,0:T(8,128)S(1)} %copy-done.1, bf16[8,128,576]{2,1,0:T(8,128)(2,1)} %bitcast.6, bf16[64,64,576]{2,1,0:T(8,128)(2,1)} %get-tuple-element.12.keys_hbm), custom_call_target="tpu_custom_call" | custom-call | tf_op jit(solution)/shard_map/attend_pages/pallas_call | solution.py:626
  27.5 0.0 copy-done
  27.5 21.9 %reduce_parts.1 = bf16[8,2048]{1,0:T(8,128)(2,1)S(1)} custom-call(bf16[8,2,4,16,512]{4,3,2,1,0:T(8,128)(2,1)S(1)} %bitcast.4, f32[8,8,128]{2,1,0:T(8,128)S(1)} %get-tuple-element.14.stat_ref, bf16[16,512,128]{2,1,0:T(8,128)(2,1)S(1)} %copy-done), custom_call_target="tpu_custom_call" | custom-call | tf_op jit(solution)/shard_map/reduce_parts/pallas_call | solution.py:653
  49.5 0.6 %copy.9 = bf16[8,2048]{1,0:T(8,128)(2,1)} copy(bf16[8,2048]{1,0:T(8,128)(2,1)S(1)} %reduce_parts.1) | data formatting | bytes 65536
Async XLA Ops:
  19.9 0.7 %copy-start.1 = (s32[8,128]{1,0:T(8,128)S(1)}, s32[8,128]{1,0:T(8,128)}, u32[]{:S(2)}) copy-start(s32[8,128]{1,0:T(8,128)} %get-tuple-element.10.meta_ref) | copy-start | bytes 12292
  20.6 6.9 %copy-start = (bf16[16,512,128]{2,1,0:T(8,128)(2,1)S(1)}, bf16[16,512,128]{2,1,0:T(8,128)(2,1)}, u32[]{:S(2)}) copy-start(bf16[16,512,128]{2,1,0:T(8,128)(2,1)} %weights_ref.1) | copy-start | bytes 6291460

commit v5 on v4

--- a/solution.py
+++ b/solution.py
@@ -152,7 +152,7 @@
     started = []
 
     def copy(a, k, b, slot, peer, send_slot=None):
-        shard = out_ref.at[pl.ds(2 * b, 2), a, k]
+        shard = out_ref.at[pl.ds(2 * b, 2), a] if k is None else out_ref.at[pl.ds(2 * b, 2), a, k]
         return pltpu.make_async_remote_copy(
             src_ref=shard,
             dst_ref=shard,
@@ -172,11 +172,11 @@
 
     Z, X, Y, D, C = 0, nrh, 2 * nrh, 3 * nrh, 4 * nrh
     half = nrh // 2
+    clump = -(-blocks // 4)
 
     def spread(k):
         push(rl, k, q, X + k, x_peer)
         push(rl, k, q, Y + k, y_peer)
-        push(rl, k, q, C + k, c_peer)
 
     for d in range(1, nrh):
         push(rl, rh, q, Z + rh, z_peer((rh + d) % nrh), send_slot=Z + d)
@@ -184,34 +184,34 @@
     load_table.wait()
     device_at = (rh * 2 + rl) * (lax.axis_size("col")) + cg * 4 + q
     list_pages(device_at, blocks * pages, length_ref, table_ref, meta_ref)
+    turn(clump)
     for d in range(1, nrh):
         k = (rh + d) % nrh
-        turn(-(-blocks // (3 * nrh)))
         arrived(rl, k, q, Z + k, z_peer(k))
         spread(k)
+    push(rl, None, q, C, c_peer)
+    turn(clump)
     for k in range(nrh):
-        turn(-(-blocks // (3 * nrh)))
         arrived(1 - rl, k, q, X + k, x_peer)
         if k >= half:
             push(1 - rl, k, q, D + k, y_peer)
-        push(1 - rl, k, q, C + nrh + k, c_peer)
         arrived(rl, k, qy, Y + k, y_peer)
         if k < half:
             push(rl, k, qy, D + k, x_peer)
-        push(rl, k, qy, C + 2 * nrh + k, c_peer)
+    push(1 - rl, None, q, C + 1, c_peer)
+    push(rl, None, qy, C + 2, c_peer)
+    turn(clump)
     for k in range(nrh):
-        turn(-(-blocks // (3 * nrh)))
         arrived(1 - rl, k, qy, D + k, x_peer if k < half else y_peer)
-        push(1 - rl, k, qy, C + 3 * nrh + k, c_peer)
+    push(1 - rl, None, qy, C + 3, c_peer)
     turn(blocks)
     for b in (q, qy):
         store(out_ref.at[pl.ds(2 * b, 2)], query_hbm.at[pl.ds(2 * b, 2)])
     qc, qyc = yl * 2 + 1 - core, (1 - yl) * 2 + 1 - core
-    for k in range(nrh):
-        arrived(rl, k, qc, C + k, c_peer)
-        arrived(1 - rl, k, qc, C + nrh + k, c_peer)
-        arrived(rl, k, qyc, C + 2 * nrh + k, c_peer)
-        arrived(1 - rl, k, qyc, C + 3 * nrh + k, c_peer)
+    arrived(rl, None, qc, C, c_peer)
+    arrived(1 - rl, None, qc, C + 1, c_peer)
+    arrived(rl, None, qyc, C + 2, c_peer)
+    arrived(1 - rl, None, qyc, C + 3, c_peer)
     for b in (qc, qyc):
         store(out_ref.at[pl.ds(2 * b, 2)], query_hbm.at[pl.ds(2 * b, 2)])
     for one in started:
@@ -339,11 +339,17 @@
 
 
 def columns(lines):
-    line = lax.broadcasted_iota(jnp.int32, (128, 128), 0)
-    table = jnp.zeros((128, 128), jnp.float32)
-    for i, one in enumerate(lines):
-        table = jnp.where(line == i, one, table)
-    return table.T
+    line = lax.broadcasted_iota(jnp.int32, (8, 128), 0)
+    tiles = []
+    for t in range(0, len(lines), 8):
+        tile = jnp.zeros((8, 128), jnp.float32)
+        for i, one in enumerate(lines[t : t + 8]):
+            tile = jnp.where(line == i, one, tile)
+        tiles.append(tile)
+    left = 128 - 8 * len(tiles)
+    if left:
+        tiles.append(jnp.zeros((left, 128), jnp.float32))
+    return jnp.concatenate(tiles, axis=0).T
 
 
 def reduce_kernel(
@@ -413,23 +419,26 @@
         top = jnp.maximum(first[0:1], second[0:1])
         one, two = jnp.exp(first[0:1] - top), jnp.exp(second[0:1] - top)
         denom = one * first[1:2] + two * second[1:2]
-        return jnp.where(line == 0, top, jnp.where(line == 1, denom, 0.0)), columns((one, two))
-
-    def merge_chunk(i, place_k, first, second):
-        weight = mix[i, pl.ds(pl.multiple_of(place_k * heads, heads), heads), :]
-        return weight[:, 0:1] * first.astype(jnp.float32) + weight[:, 1:2] * second.astype(
-            jnp.float32
-        )
+        return jnp.where(line == 0, top, jnp.where(line == 1, denom, 0.0)), [one, two]
+
+    def merge_chunk(n, place_k, first, second):
+        weight = mix[pl.ds(pl.multiple_of(place_k * heads, heads), heads), :]
+        one, two = weight[:, 2 * n : 2 * n + 1], weight[:, 2 * n + 1 : 2 * n + 2]
+        return one * first.astype(jnp.float32) + two * second.astype(jnp.float32)
 
     stat_in.wait_recv()
+    weights = []
+    for side in range(2):
+        stats = y_stat if side == 0 else own_stat
+        for i in range(2):
+            r = 2 * (2 * (1 - yl if side == 0 else yl) + core) + i
+            stats[i], pair = merge_stats(stat_ref[r], core_stat[r])
+            weights += pair
+        if side == 0:
+            push(y_stat, y_stat_in, 3, y_peer)
+    mix[...] = columns(weights)
     for side in range(2):
         y = 1 - yl if side == 0 else yl
-        stats = y_stat if side == 0 else own_stat
-        for i in range(2):
-            r = 2 * (2 * y + core) + i
-            stats[i], mix[i] = merge_stats(stat_ref[r], core_stat[r])
-        if side == 0:
-            push(y_stat, y_stat_in, 3, y_peer)
         if side == 1:
             own_in.wait_recv()
         for d in range(1, nrow + 1):
@@ -439,7 +448,9 @@
                 core_in[d - 1].wait_recv()
             for i in range(2):
                 r = 2 * (2 * y + core) + i
-                merged = merge_chunk(i, place_k, part_ref[r, a, k], core_part[side, i, a, k])
+                merged = merge_chunk(
+                    2 * side + i, place_k, part_ref[r, a, k], core_part[side, i, a, k]
+                )
                 if side == 0:
                     y_send[a, k, i] = merged.astype(y_send.dtype)
                 else:
@@ -448,8 +459,11 @@
                 push(y_send.at[a, k], y_part.at[a, k], 3 + d, y_peer)
 
     remote(y_stat, y_stat_in, 3, y_peer).wait_recv()
+    weights = []
     for i in range(2):
-        row_stat[i], mix[i] = merge_stats(own_stat[i], y_stat_in[i])
+        row_stat[i], pair = merge_stats(own_stat[i], y_stat_in[i])
+        weights += pair
+    mix[...] = columns(weights)
 
     def row_copies(to, source, d):
         return (
@@ -482,37 +496,6 @@
 
     my_heads = pl.ds(pl.multiple_of((rl * nrh + rh) * heads, heads), heads)
 
-    def weigh():
-        def take_stat(d, carry):
-            row_copies(me, (me + d) % spots, d)[1].wait_recv()
-            return carry
-
-        lax.fori_loop(1, spots, take_stat, 0)
-        def top_step(s, tops):
-            new = []
-            for i in range(2):
-                new.append(jnp.maximum(tops[i], row_stat_in[s, i][0:1]))
-            return tuple(new)
-
-        tops = lax.fori_loop(0, spots, top_step, (jnp.full((1, 128), MASKED, jnp.float32),) * 2)
-
-        def denom_step(s, denoms):
-            return tuple(
-                denoms[i] + jnp.exp(row_stat_in[s, i][0:1] - tops[i]) * row_stat_in[s, i][1:2]
-                for i in range(2)
-            )
-
-        denoms = lax.fori_loop(0, spots, denom_step, (jnp.zeros((1, 128), jnp.float32),) * 2)
-        for i in range(2):
-            lines[0, i] = columns((denoms[i],))
-
-        def weight_step(s, carry):
-            for i in range(2):
-                lines[1 + s, i] = columns((jnp.exp(row_stat_in[s, i][0:1] - tops[i]),))
-            return carry
-
-        lax.fori_loop(0, spots, weight_step, 0)
-
     for d in range(1, nrow + 1):
         place_k = (rl * nrh + rh + d) % nrow
         chunk_step(place_k, d)
@@ -529,7 +512,24 @@
         lax.fori_loop(0, ncg, send_chunk, 0)
     row_part[me] = row_send[me // ncg]
 
-    weigh()
+    def take_stat(d, carry):
+        row_copies(me, (me + d) % spots, d)[1].wait_recv()
+        return carry
+
+    lax.fori_loop(1, spots, take_stat, 0)
+    weights, denoms = [], []
+    for i in range(2):
+        parts = [(row_stat_in[n, i][0:1], row_stat_in[n, i][1:2]) for n in range(spots)]
+        top = functools.reduce(jnp.maximum, [one for one, _ in parts])
+        shares = [jnp.exp(one - top) for one, _ in parts]
+        denoms.append(sum(share * denom for share, (_, denom) in zip(shares, parts)))
+        weights += shares
+    weights += denoms
+    for n in range(0, len(weights), 128):
+        lines[n // 128] = columns(weights[n : n + 128])
+
+    def column(n):
+        return lines[n // 128, my_heads, :][:, n % 128 : n % 128 + 1]
 
     def take_part(d, carry):
         row_copies(me, (me + d) % spots, d)[0].wait_recv()
@@ -537,17 +537,11 @@
 
     lax.fori_loop(1, spots, take_part, 0)
 
-    def sum_step(s, sums):
-        return tuple(
-            sums[i]
-            + lines[1 + s, i, my_heads, :][:, 0:1] * row_part[s, i].astype(jnp.float32)
-            for i in range(2)
-        )
-
-    width = row_part.shape[-1]
-    sums = lax.fori_loop(0, spots, sum_step, (jnp.zeros((heads, width), jnp.float32),) * 2)
     for i in range(2):
-        value[i * heads : (i + 1) * heads, :] = sums[i] / lines[0, i, my_heads, :][:, 0:1]
+        total = sum(
+            column(i * spots + n) * row_part[n, i].astype(jnp.float32) for n in range(spots)
+        )
+        value[i * heads : (i + 1) * heads, :] = total / column(2 * spots + i)
     rows = value[...].astype(jnp.bfloat16)
 
     shared[q] = head_diagonal(rows, weights_ref, heads).reshape(2, heads, shared.shape[3])
@@ -607,7 +601,7 @@
             pltpu.VMEM((slots, PAGE, full), jnp.bfloat16),
             pltpu.SemaphoreType.DMA((4 + CACHE_LOADS,)),
             pltpu.SemaphoreType.DMA((4 + slots * PAGE // (BLOCK * STORED),)),
-            pltpu.SemaphoreType.DMA((8 * nrh,)), pltpu.SemaphoreType.DMA((8 * nrh,))],
+            pltpu.SemaphoreType.DMA((4 * nrh + 4,)), pltpu.SemaphoreType.DMA((4 * nrh + 4,))],
         compiler_params=pltpu.CompilerParams(
             collective_id=0, has_side_effects=True, vmem_limit_bytes=VMEM_LIMIT
         ),
@@ -671,8 +665,8 @@
             pltpu.VMEM((2, 8, all_heads), f32),
             pltpu.VMEM((spots, 2, heads, width), wire),
             pltpu.VMEM((spots, 2, 8, all_heads), f32),
-            pltpu.VMEM((2, 128, 128), f32),
-            pltpu.VMEM((spots + 1, 2, 128, 128), f32),
+            pltpu.VMEM((128, 128), f32),
+            pltpu.VMEM((-(-(2 * spots + 2) // 128), 128, 128), f32),
             pltpu.VMEM((2 * heads, width), f32),
             pltpu.SemaphoreType.DMA((7 + 2 * nrow,)),
             pltpu.SemaphoreType.DMA((7 + 2 * nrow,)),

time: 50.2 us -> 48.7 us (0.970)
  Pallas kernels: 48.8 us -> 47.4 us
    pallas_call x1, Pallas kernels: 21.9 us -> 20.1 us  [local(): pl.pallas_call(functools.partial(reduce_kernel, nrh, ncg, heads), out_sha...]
where the time goes in v5:
time: 48.7 us
  Pallas kernels  47.4 us (97%)
  local copies, waits for them, and re-layouts  1.29 us (3%)
    pallas_call x1, Pallas kernels, local(): pl.pallas_call(functools.partial(gather_kernel, nrh, heads), out_shape=(j...  20.3 us
    pallas_call x1, Pallas kernels, local(): pl.pallas_call(functools.partial(reduce_kernel, nrh, ncg, heads), out_sha...  20.1 us
    pallas_call x1, Pallas kernels, local(): pl.pallas_call(functools.partial(attend_kernel, scale), out_shape=(jax.Sh...  6.92 us
    unnamed x5, local copies, waits for them, and re-layouts  1.29 us

profile of v5, /device:TPU:0, one launch (start us, length us, event | category | flops | bytes accessed | tf_op | source)
XLA Modules:
  0.0 48.7 jit_solution(5193131926074194656)
XLA Ops:
  0.0 20.3 %gather_queries.1 = (bf16[8,2,4,16,576]{4,3,2,1,0:T(8,128)(2,1)}, bf16[64,64,576]{2,1,0:T(8,128)(2,1)}, s32[8,128]{1,0:T(8,128)}) custom-call(s32[8]{0:T(128)} %length_ref.1, bf16[128,128]{1,0:T(8,128)(2,1)} %bitcast.7, bf16[8,16,64]{2,1,0:T(8,128)(2,1)} %rope_hbm.1, bf16[16,128,512]{2,1,0:T(8,128)(2,1)} %weights_hbm.1, bf16[576,4096]{1,0:T(8,128)(2,1)} %bitcast.5, ...), custom_call_target="tpu_custom_call" | custom-call | tf_op jit(solution)/shard_map/gather_queries/pallas_call | solution.py:585
  20.3 0.0 copy-start.1
  20.3 0.7 %copy-done.1 = s32[8,128]{1,0:T(8,128)S(1)} copy-done((s32[8,128]{1,0:T(8,128)S(1)}, s32[8,128]{1,0:T(8,128)}, u32[]{:S(2)}) %copy-start.1) | copy-done | bytes 4120
  21.0 0.0 copy-start
  21.0 6.9 %attend_pages.1 = (bf16[8,128,512]{2,1,0:T(8,128)(2,1)S(1)}, f32[8,8,128]{2,1,0:T(8,128)S(1)}) custom-call(s32[8,128]{1,0:T(8,128)S(1)} %copy-done.1, bf16[8,128,576]{2,1,0:T(8,128)(2,1)} %bitcast.6, bf16[64,64,576]{2,1,0:T(8,128)(2,1)} %get-tuple-element.12.keys_hbm), custom_call_target="tpu_custom_call" | custom-call | tf_op jit(solution)/shard_map/attend_pages/pallas_call | solution.py:620
  27.9 0.0 copy-done
  27.9 20.1 %reduce_parts.1 = bf16[8,2048]{1,0:T(8,128)(2,1)S(1)} custom-call(bf16[8,2,4,16,512]{4,3,2,1,0:T(8,128)(2,1)S(1)} %bitcast.4, f32[8,8,128]{2,1,0:T(8,128)S(1)} %get-tuple-element.14.stat_ref, bf16[16,512,128]{2,1,0:T(8,128)(2,1)S(1)} %copy-done), custom_call_target="tpu_custom_call" | custom-call | tf_op jit(solution)/shard_map/reduce_parts/pallas_call | solution.py:647
  48.1 0.6 %copy.9 = bf16[8,2048]{1,0:T(8,128)(2,1)} copy(bf16[8,2048]{1,0:T(8,128)(2,1)S(1)} %reduce_parts.1) | data formatting | bytes 65536
Async XLA Ops:
  20.3 0.7 %copy-start.1 = (s32[8,128]{1,0:T(8,128)S(1)}, s32[8,128]{1,0:T(8,128)}, u32[]{:S(2)}) copy-start(s32[8,128]{1,0:T(8,128)} %get-tuple-element.10.meta_ref) | copy-start | bytes 12292
  21.0 6.9 %copy-start = (bf16[16,512,128]{2,1,0:T(8,128)(2,1)S(1)}, bf16[16,512,128]{2,1,0:T(8,128)(2,1)}, u32[]{:S(2)}) copy-start(bf16[16,512,128]{2,1,0:T(8,128)(2,1)} %weights_ref.1) | copy-start | bytes 6291460

commit v6 on v5

--- a/solution.py
+++ b/solution.py
@@ -15,6 +15,7 @@
 BLOCK = 128
 CACHE_LOADS = 4
 STORED = 4
+LIST_ROWS = 8192
 MASKED = -1e30
 MESH = pl.DeviceIdType.MESH
 VMEM_LIMIT = 62 * 1024 * 1024
@@ -29,11 +30,12 @@
     return (rh * 2 + rl, cg * 4 + yl * 2 + core)
 
 
-def head_diagonal(rows, weights_ref, heads):
+def head_diagonal(rows, weights_ref, heads, ready=lambda h: None):
     count = rows.shape[0]
     head = lax.broadcasted_iota(jnp.int32, (count, weights_ref.shape[2]), 0) % heads
     total = jnp.zeros((count, weights_ref.shape[2]), jnp.float32)
     for h in range(heads):
+        ready(h)
         product = jnp.dot(rows, weights_ref[h], preferred_element_type=jnp.float32)
         total = jnp.where(head == h, product, total)
     return total
@@ -80,7 +82,7 @@
 
 def gather_kernel(
     nrh, heads, length_ref, nope_hbm, rope_hbm, weights_hbm, cache_hbm, table_hbm,
-    query_hbm, keys_hbm, meta_ref,
+    query_hbm, keys_hbm, meta_hbm, meta_ref,
     nope_ref, rope_ref, weights_ref, cache_ref, table_ref, out_ref, keys_ref,
     local_sem, store_sem, send, recv,
 ):
@@ -100,7 +102,14 @@
     loads = [
         pltpu.make_async_copy(nope_hbm, nope_ref, local_sem.at[0]),
         pltpu.make_async_copy(rope_hbm, rope_ref, local_sem.at[1]),
-        pltpu.make_async_copy(weights_hbm, weights_ref, local_sem.at[2]),
+    ]
+    quarter = heads // 4
+    weight_loads = [
+        pltpu.make_async_copy(
+            weights_hbm.at[pl.ds(n * quarter, quarter)], weights_ref.at[pl.ds(n * quarter, quarter)],
+            local_sem.at[4 + CACHE_LOADS + n],
+        )
+        for n in range(4)
     ]
     span = cache_hbm.shape[1] // CACHE_LOADS
     cache_loads = [
@@ -111,7 +120,7 @@
         for j in range(CACHE_LOADS)
     ]
     load_table = pltpu.make_async_copy(table_hbm, table_ref, local_sem.at[3 + CACHE_LOADS])
-    for one in loads + [load_table]:
+    for one in loads + weight_loads + [load_table]:
         one.start()
     stores = []
 
@@ -138,10 +147,16 @@
 
     for one in loads:
         one.wait()
-    for one in cache_loads:
-        one.start()
+
+    def ready(h):
+        if h % quarter == 0:
+            weight_loads[h // quarter].wait()
+        if h == 3 * quarter:
+            for one in cache_loads:
+                one.start()
+
     rows = nope_ref[pl.ds(pl.multiple_of(q * 2 * heads, 2 * heads), 2 * heads), :]
-    latent = head_diagonal(rows.astype(jnp.bfloat16), weights_ref, heads)
+    latent = head_diagonal(rows.astype(jnp.bfloat16), weights_ref, heads, ready)
     latent = latent.astype(jnp.bfloat16).astype(out_ref.dtype)
     width = weights_ref.shape[2]
     for i in range(2):
@@ -170,6 +185,9 @@
     def arrived(a, k, b, slot, peer):
         copy(a, k, b, slot, peer).wait_recv()
 
+    def put(a, b):
+        store(out_ref.at[pl.ds(2 * b, 2), a], query_hbm.at[pl.ds(2 * b, 2), a])
+
     Z, X, Y, D, C = 0, nrh, 2 * nrh, 3 * nrh, 4 * nrh
     half = nrh // 2
     clump = -(-blocks // 4)
@@ -184,12 +202,14 @@
     load_table.wait()
     device_at = (rh * 2 + rl) * (lax.axis_size("col")) + cg * 4 + q
     list_pages(device_at, blocks * pages, length_ref, table_ref, meta_ref)
+    store(meta_ref, meta_hbm.at[pl.ds(0, 8)])
     turn(clump)
     for d in range(1, nrh):
         k = (rh + d) % nrh
         arrived(rl, k, q, Z + k, z_peer(k))
         spread(k)
     push(rl, None, q, C, c_peer)
+    put(rl, q)
     turn(clump)
     for k in range(nrh):
         arrived(1 - rl, k, q, X + k, x_peer)
@@ -200,20 +220,18 @@
             push(rl, k, qy, D + k, x_peer)
     push(1 - rl, None, q, C + 1, c_peer)
     push(rl, None, qy, C + 2, c_peer)
+    put(1 - rl, q)
+    put(rl, qy)
     turn(clump)
     for k in range(nrh):
         arrived(1 - rl, k, qy, D + k, x_peer if k < half else y_peer)
     push(1 - rl, None, qy, C + 3, c_peer)
     turn(blocks)
-    for b in (q, qy):
-        store(out_ref.at[pl.ds(2 * b, 2)], query_hbm.at[pl.ds(2 * b, 2)])
+    put(1 - rl, qy)
     qc, qyc = yl * 2 + 1 - core, (1 - yl) * 2 + 1 - core
-    arrived(rl, None, qc, C, c_peer)
-    arrived(1 - rl, None, qc, C + 1, c_peer)
-    arrived(rl, None, qyc, C + 2, c_peer)
-    arrived(1 - rl, None, qyc, C + 3, c_peer)
-    for b in (qc, qyc):
-        store(out_ref.at[pl.ds(2 * b, 2)], query_hbm.at[pl.ds(2 * b, 2)])
+    for n, (a, b) in enumerate(((rl, qc), (1 - rl, qc), (rl, qyc), (1 - rl, qyc))):
+        arrived(a, None, b, C + n, c_peer)
+        put(a, b)
     for one in started:
         one.wait_send()
     for one in stores:
@@ -221,12 +239,16 @@
 
 
 def attend_kernel(
-    scale, meta_ref, query_hbm, keys_hbm, part_ref, stat_ref,
-    query_ref, keys_ref, scores, tops, denoms, total, owner, start, query_sem, page_sem,
+    scale, meta_hbm, query_hbm, keys_hbm, part_ref, stat_ref,
+    meta_ref, query_ref, keys_ref, scores, tops, denoms, total, owner, start,
+    query_sem, page_sem,
 ):
     requests, heads, _ = query_ref.shape
     width = part_ref.shape[2]
-    held = meta_ref[2, requests]
+    fetch_lists = pltpu.make_async_copy(
+        meta_hbm.at[pl.ds(0, 8)], meta_ref, query_sem.at[requests]
+    )
+    fetch_lists.start()
 
     def fetch(k):
         return pltpu.make_async_copy(
@@ -244,11 +266,14 @@
         fetch(k).wait()
         return carry
 
-    fetch_query(0).start()
-    lax.fori_loop(0, jnp.minimum(held, 2 * GROUP), start_fetch, 0)
-    for r in range(1, requests):
+    for r in range(requests):
         fetch_query(r).start()
-    lax.fori_loop(jnp.minimum(held, 2 * GROUP), held, start_fetch, 0)
+    tops[...] = jnp.full(tops.shape, MASKED, jnp.float32)
+    denoms[...] = jnp.zeros(denoms.shape, jnp.float32)
+    total[...] = jnp.zeros(total.shape, jnp.float32)
+    fetch_lists.wait()
+    held = meta_ref[2, requests]
+    lax.fori_loop(0, held, start_fetch, 0)
     for i in range(GROUP):
         keys_ref[held + i] = jnp.zeros(keys_ref.shape[1:], keys_ref.dtype)
 
@@ -269,20 +294,21 @@
         owner[count + i] = requests
         start[count + i] = 0
     rounds = (count + PAIR - 1) // PAIR
-
-    tops[...] = jnp.full(tops.shape, MASKED, jnp.float32)
-    denoms[...] = jnp.zeros(denoms.shape, jnp.float32)
-    total[...] = jnp.zeros(total.shape, jnp.float32)
     token = lax.broadcasted_iota(jnp.int32, (PAGE, heads), 0)
 
     def pages(at, columns_kept):
         rows = keys_ref[pl.ds(at, GROUP), :, 0:columns_kept]
         return rows.reshape(GROUP * PAGE, columns_kept)
 
-    for r in range(requests):
+    def end_query(r, carry):
         fetch_query(r).wait()
-
-    def score_round(n, here):
+        return carry
+
+    def score_round(n, carry):
+        here, asked = carry
+        wanted = jnp.maximum(owner[n * PAIR], owner[n * PAIR + PAIR - 1]) + 1
+        wanted = jnp.minimum(wanted, requests)
+        lax.fori_loop(asked, wanted, end_query, 0)
         need = jnp.maximum(start[n * PAIR], start[n * PAIR + PAIR - 1]) + GROUP
         need = jnp.maximum(jnp.minimum(need, held), here)
         lax.fori_loop(here, need, end_fetch, 0)
@@ -309,10 +335,11 @@
                 scores[g, rows, :] = piece
                 top = jnp.maximum(top, jnp.max(piece, axis=0, keepdims=True))
             tops[r] = top
-        return need
-
-    here = lax.fori_loop(0, rounds, score_round, 0)
+        return need, wanted
+
+    here, asked = lax.fori_loop(0, rounds, score_round, (0, 0))
     lax.fori_loop(here, held, end_fetch, 0)
+    lax.fori_loop(asked, requests, end_query, 0)
 
     def sum_round(n, carry):
         products = []
@@ -587,11 +614,12 @@
         out_shape=(
             jax.ShapeDtypeStruct((requests, 2, nrh, heads, full), wire),
             jax.ShapeDtypeStruct((slots, PAGE, full), jnp.bfloat16),
-            jax.ShapeDtypeStruct((8, 128), jnp.int32),
+            jax.ShapeDtypeStruct((LIST_ROWS, 128), jnp.int32),
         ),
         in_specs=[smem] + [hbm] * 5,
-        out_specs=(hbm, hbm, vmem),
+        out_specs=(hbm, hbm, hbm),
         scratch_shapes=[
+            pltpu.VMEM((8, 128), jnp.int32),
             pltpu.VMEM((requests * heads, nope), wire),
             pltpu.VMEM(query_rope.shape, wire),
             pltpu.VMEM(key_up_weight.shape, jnp.bfloat16),
@@ -599,8 +627,8 @@
             pltpu.VMEM(page_table.shape, jnp.int32),
             pltpu.VMEM((requests, 2, nrh, heads, full), wire),
             pltpu.VMEM((slots, PAGE, full), jnp.bfloat16),
-            pltpu.SemaphoreType.DMA((4 + CACHE_LOADS,)),
-            pltpu.SemaphoreType.DMA((4 + slots * PAGE // (BLOCK * STORED),)),
+            pltpu.SemaphoreType.DMA((8 + CACHE_LOADS,)),
+            pltpu.SemaphoreType.DMA((9 + slots * PAGE // (BLOCK * STORED),)),
             pltpu.SemaphoreType.DMA((4 * nrh + 4,)), pltpu.SemaphoreType.DMA((4 * nrh + 4,))],
         compiler_params=pltpu.CompilerParams(
             collective_id=0, has_side_effects=True, vmem_limit_bytes=VMEM_LIMIT
@@ -623,9 +651,10 @@
             jax.ShapeDtypeStruct((requests, all_heads, width), wire),
             jax.ShapeDtypeStruct((requests, 8, all_heads), jnp.float32),
         ),
-        in_specs=[smem, hbm, hbm],
+        in_specs=[hbm, hbm, hbm],
         out_specs=(vmem, vmem),
         scratch_shapes=[
+            pltpu.SMEM((8, 128), jnp.int32),
             pltpu.VMEM((requests, all_heads, full), jnp.bfloat16),
             pltpu.VMEM((slots + GROUP, PAGE, full), jnp.bfloat16),
             pltpu.VMEM((most, GROUP * PAGE, all_heads), jnp.float32),
@@ -634,7 +663,7 @@
             pltpu.VMEM((requests + 1, all_heads, width), jnp.float32),
             pltpu.SMEM((most,), jnp.int32),
             pltpu.SMEM((most,), jnp.int32),
-            pltpu.SemaphoreType.DMA((requests,)),
+            pltpu.SemaphoreType.DMA((requests + 1,)),
             pltpu.SemaphoreType.DMA((slots,)),
         ],
         compiler_params=pltpu.CompilerParams(vmem_limit_bytes=52 * 1024 * 1024),

time: 48.7 us -> 48 us (0.986)
  local copies, waits for them, and re-layouts: 1.29 us -> 0.62 us
    pallas_call x1, Pallas kernels: 20.3 us -> 19.5 us  [local(): pl.pallas_call(functools.partial(gather_kernel, nrh, heads), out_shape=(j...]
    unnamed x5 -> x3, local copies, waits for them, and re-layouts: 1.29 us -> 0.62 us
    pallas_call x1, Pallas kernels: 20.1 us -> 20.6 us  [local(): pl.pallas_call(functools.partial(reduce_kernel, nrh, ncg, heads), out_sha...]
where the time goes in v6:
time: 48 us; the launch traced here: 47.6 us
  Pallas kernels  47 us (98%)
  local copies, waits for them, and re-layouts  0.62 us (1%)
    pallas_call x1, Pallas kernels, local(): pl.pallas_call(functools.partial(reduce_kernel, nrh, ncg, heads), out_sha...  20.6 us
    pallas_call x1, Pallas kernels, local(): pl.pallas_call(functools.partial(gather_kernel, nrh, heads), out_shape=(j...  19.5 us
    pallas_call x1, Pallas kernels, local(): pl.pallas_call(functools.partial(attend_kernel, scale), out_shape=(jax.Sh...  6.82 us

profile of v6, /device:TPU:0, one launch (start us, length us, event | category | flops | bytes accessed | tf_op | source)
XLA Modules:
  0.0 47.6 jit_solution(10308496906609345449)
XLA Ops:
  0.0 19.5 %gather_queries.1 = (bf16[8,2,4,16,576]{4,3,2,1,0:T(8,128)(2,1)}, bf16[64,64,576]{2,1,0:T(8,128)(2,1)}, s32[8192,128]{1,0:T(8,128)}) custom-call(s32[8]{0:T(128)} %length_ref.1, bf16[128,128]{1,0:T(8,128)(2,1)} %bitcast.7, bf16[8,16,64]{2,1,0:T(8,128)(2,1)} %rope_hbm.1, bf16[16,128,512]{2,1,0:T(8,128)(2,1)} %weights_hbm.1, bf16[576,4096]{1,0:T(8,128)(2,1)} %bitcast.5, ...), custom_call_target="tpu_custom_call" | custom-call | tf_op jit(solution)/shard_map/gather_queries/pallas_call | solution.py:612
  19.5 0.0 copy-start
  19.5 6.8 %attend_pages.1 = (bf16[8,128,512]{2,1,0:T(8,128)(2,1)S(1)}, f32[8,8,128]{2,1,0:T(8,128)S(1)}) custom-call(s32[8192,128]{1,0:T(8,128)} %get-tuple-element.10.meta_hbm, bf16[8,128,576]{2,1,0:T(8,128)(2,1)} %bitcast.6, bf16[64,64,576]{2,1,0:T(8,128)(2,1)} %get-tuple-element.12.keys_hbm), custom_call_target="tpu_custom_call" | custom-call | tf_op jit(solution)/shard_map/attend_pages/pallas_call | solution.py:648
  26.4 0.0 copy-done
  26.4 20.6 %reduce_parts.1 = bf16[8,2048]{1,0:T(8,128)(2,1)S(1)} custom-call(bf16[8,2,4,16,512]{4,3,2,1,0:T(8,128)(2,1)S(1)} %bitcast.4, f32[8,8,128]{2,1,0:T(8,128)S(1)} %get-tuple-element.14.stat_ref, bf16[16,512,128]{2,1,0:T(8,128)(2,1)S(1)} %copy-done), custom_call_target="tpu_custom_call" | custom-call | tf_op jit(solution)/shard_map/reduce_parts/pallas_call | solution.py:676
  47.0 0.6 %copy.9 = bf16[8,2048]{1,0:T(8,128)(2,1)} copy(bf16[8,2048]{1,0:T(8,128)(2,1)S(1)} %reduce_parts.1) | data formatting | bytes 65536
Async XLA Ops:
  19.5 6.8 %copy-start = (bf16[16,512,128]{2,1,0:T(8,128)(2,1)S(1)}, bf16[16,512,128]{2,1,0:T(8,128)(2,1)}, u32[]{:S(2)}) copy-start(bf16[16,512,128]{2,1,0:T(8,128)(2,1)} %weights_ref.1) | copy-start | bytes 6291460
